TPU v7x, 256 devices: a whole 4x4x8 slice. The times are simulated.
256 devices in a mesh: group: 8 (over z), shard: 32 (over y, x, core).
Axes of the slice: x: 4, y: 4, z: 8, core: 2. Of those that a mesh axis runs over, the one named last changes fastest.
Arguments:
- queries: bfloat16 [8, 512, 2048], P('group', 'shard'), may hold values from -6 to 6
- fine_codebook: bfloat16 [256, 2048], replicated, may hold values from -0.125 to 0.125
- coarse_codebook: bfloat16 [256, 64], replicated, may hold values from -0.75 to 0.75
- fine_codes: int32 [64, 256, 256], P('shard'), may hold values from 0 to 255
- coarse_codes: int32 [8, 32768], P(None, 'group'), may hold values from 0 to 255
- shortlist: int32 [8, 512, 8], P('group', 'shard'), may hold values from 0 to 63, all different within a row; in each aligned block of 16 rows (0 to 15, 16 to 31, ..., all dimensions but the last counted through in order) at most 4 rows name the same one
- owner: int32 [64], replicated, may hold values from 0 to 63, each once
- block_counts: int32 [64], P('shard'), may hold values from 1 to 2
Outputs:
- coarse_scores: float32 [8, 512, 32768], P(None, 'shard', 'group')
- fine_scores: float32 [8, 512, 8, 256], P('group', 'shard')
Inputs may be any that keep to these rules, and one draw needn't show every extreme that they name: `shortlist`: the 8 clusters of one query differ. Among the queries of one device (aligned blocks of 16 queries) no cluster is named by more than 4 of them, a bound that some block reaches. A permutation: cluster c is stored at slot owner[c].
All inputs are finite; a program needn't handle non-finite values.
Results may differ from a plain program's by a relative error of at most 0.0029.
Values may be sent and summed in bfloat16 or wider, within the bound.
No kernel may reach another device: no remote copies, remote signals or barrier semaphores. Data moves between devices by JAX's collectives and lax.ppermute only.
A program may use at most 128 MiB of HBM per device.

v0:
```python
import jax
import jax.numpy as jnp
from jax import lax
from jax.sharding import PartitionSpec as P

PREFIX = 64
MC = 8
BLOCK = 128


def build_tables(vectors_cols, codebook_cols, subspaces):
    width = vectors_cols.shape[0]
    vector_count = vectors_cols.shape[1]
    centers = codebook_cols.shape[1]
    stride = width // subspaces
    pieces = vectors_cols.reshape(subspaces, stride, vector_count)
    entries = codebook_cols.reshape(subspaces, stride, centers)
    tables = jnp.einsum("mjn,mjk->mkn", pieces, entries, preferred_element_type=jnp.float32)
    return tables.astype(jnp.bfloat16).reshape(subspaces * centers, vector_count)


def score_codes(tables, code_rows, group_size):
    subspaces = code_rows.shape[0]
    length = code_rows.shape[1]
    centers = tables.shape[0] // subspaces
    levels = jnp.arange(centers, dtype=jnp.int32)

    def one_step(step_index, running):
        code_block = lax.dynamic_slice_in_dim(code_rows, step_index * group_size, group_size, 0)
        onehot = (
            (code_block[:, None, :] == levels[None, :, None])
            .astype(jnp.bfloat16)
            .reshape(group_size * centers, length)
        )
        part_tables = lax.dynamic_slice_in_dim(
            tables, step_index * group_size * centers, group_size * centers, 0
        )
        product = lax.dot_general(
            part_tables, onehot, (((0,), (0,)), ((), ())), preferred_element_type=jnp.float32
        )
        return running + product

    zero_sums = jnp.zeros((tables.shape[1], length), jnp.float32)
    return lax.fori_loop(0, subspaces // group_size, one_step, zero_sums)


def body(
    queries,
    fine_codebook,
    coarse_codebook,
    fine_codes,
    coarse_codes,
    shortlist,
    owner,
    block_counts,
):
    shards = lax.axis_size("shard")
    groups = lax.axis_size("group")
    local_count = fine_codes.shape[0]
    subspaces = fine_codes.shape[1]
    row_count = fine_codes.shape[2]
    per_device = queries.shape[1]
    feature_width = queries.shape[2]
    probes = shortlist.shape[2]
    clusters = owner.shape[0]
    capacity = max(2, 2 * per_device * probes // clusters)
    positions = local_count * shards * capacity
    coarse_cols = coarse_codebook.T
    own_tables = build_tables(queries[0, :, :PREFIX].T, coarse_cols, MC)
    coarse_tables = lax.all_gather(own_tables, "group", axis=1, tiled=True)
    slab_rows = coarse_codes.shape[1]
    block_span = min(1024, slab_rows)

    def coarse_block(block_index, scores):
        code_block = lax.dynamic_slice_in_dim(coarse_codes, block_index * block_span, block_span, 1)
        return lax.dynamic_update_slice_in_dim(
            scores, score_codes(coarse_tables, code_block, MC), block_index * block_span, 1
        )

    coarse_scores = lax.fori_loop(
        0,
        slab_rows // block_span,
        coarse_block,
        jnp.zeros((groups * per_device, slab_rows), jnp.float32),
    )
    coarse_scores = coarse_scores.reshape(groups, per_device, slab_rows)
    my_lists = shortlist[0].reshape(-1)
    item_count = my_lists.shape[0]
    cluster_ids = jnp.arange(clusters, dtype=jnp.int32)
    storage = jnp.sum(
        jnp.where(my_lists[:, None] == cluster_ids[None, :], owner[None, :], 0), axis=1
    )
    item_ids = jnp.arange(item_count, dtype=jnp.int32)
    earlier = (my_lists[:, None] == my_lists[None, :]) & (item_ids[:, None] > item_ids[None, :])
    ranking = jnp.sum(earlier.astype(jnp.int32), axis=1)
    target = (
        storage % local_count * (shards * capacity) + storage // local_count * capacity + ranking
    )
    slot_ids = jnp.arange(positions, dtype=jnp.int32)
    chosen = target.reshape(per_device, probes)[None, :, :] == slot_ids[:, None, None]
    routing = jnp.sum(chosen.astype(jnp.float32), axis=2).astype(jnp.bfloat16)
    outgoing = jnp.dot(routing, queries[0], preferred_element_type=jnp.float32).astype(jnp.bfloat16)
    arrived = lax.all_to_all(
        outgoing.reshape(local_count, shards, capacity, feature_width),
        "shard",
        split_axis=1,
        concat_axis=1,
        tiled=True,
    )
    fine_cols = fine_codebook.T
    row_ids = jnp.arange(row_count, dtype=jnp.int32)
    results = []
    for local_id in range(local_count):
        item_rows = arrived[local_id].reshape(shards * capacity, feature_width)
        fine_tables = build_tables(item_rows.T, fine_cols, subspaces)
        scores = score_codes(fine_tables, fine_codes[local_id], min(32, subspaces))
        row_limit = BLOCK * block_counts[local_id]
        results.append(jnp.where(row_ids[None, :] < row_limit, scores, jnp.zeros_like(scores)))
    computed = jnp.stack(results).reshape(local_count, shards, capacity, row_count)
    returned = lax.all_to_all(computed, "shard", split_axis=1, concat_axis=1, tiled=True)
    fine_scores = jnp.take(returned.reshape(positions, row_count), target, axis=0)
    return (coarse_scores, fine_scores.reshape(1, per_device, probes, row_count))


def solution(mesh):
    in_specs = (
        P("group", "shard", None),
        P(),
        P(),
        P("shard", None, None),
        P(None, "group"),
        P("group", "shard", None),
        P(),
        P("shard"),
    )
    out_specs = (P(None, "shard", "group"), P("group", "shard", None, None))
    return jax.shard_map(body, mesh=mesh, in_specs=in_specs, out_specs=out_specs, check_vma=False)
```

profile of v0, /device:TPU:1, one launch (start us, length us, event | category | flops | bytes accessed | tf_op | source)
XLA Modules:
  0.0 240.9 jit_solution(7655567996962831385)
XLA Ops:
  6.1 8.6 %all-to-all-start = ((bf16[2,32,4,2048]{3,2,0,1:T(4,128)(2,1)}), bf16[2,32,4,2048]{3,2,0,1:T(4,128)(2,1)S(1)}, u32[]{:S(2)}, u32[]{:S(2)}) async-start(bf16[2,32,4,2048]{3,2,0,1:T(4,128)(2,1)} %copy.44), calls=%async_computation | async-start | bytes 2097152 | tf_op jit(solution)/shard_map/all_to_all | solution.py:103
  15.7 24.2 %all_gather.3 = bf16[2048,128]{0,1:T(8,128)(2,1)S(1)} all-gather(bf16[2048,16]{0,1:T(8,128)(2,1)S(1)} %bitcast.131), channel_id=1, replica_groups=mesh['group'=8,'shard'=32] {'group'}, dimensions={1}, use_global_device_ids=true | all-gather | bytes 589824 | tf_op jit(solution)/shard_map/all_gather | solution.py:70
  41.7 22.1 %while.54 = (s32[]{:T(128)}, f32[128,4096]{1,0:T(8,128)}, s32[8,4096]{1,0:T(8,128)}, bf16[2048,128]{1,0:T(8,128)(2,1)S(1)}, s32[]{:T(128)}, /*index=5*/s32[]{:T(128)}, s32[]{:T(128)}, s32[]{:T(128)}) while((s32[]{:T(128)}, f32[128,4096]{1,0:T(8,128)}, s32[8,4096]{1,0:T(8,128)}, bf16[2048,128]{1,0:T(8,128)(2,1)S(1)}, s32[]{:T(128)}, ...), condition=%wide.region_1.2_spmd, body=%wide.region_0.1_spmd.sunk | while | flops 538968064 | bytes 7471243 | solution.py:80
  69.9 8.1 %convert_bitcast_fusion = bf16[256,256,128]{1,2,0:T(8,128)(2,1)} fusion(bf16[256,2048]{0,1:T(8,128)(2,1)S(1)} %copy.46, bf16[128,2048]{0,1:T(8,128)(2,1)S(1)} %copy.48), kind=kOutput, calls=%fused_computation.22 | convolution fusion | flops 142606336 | bytes 18350080 | tf_op jit(solution)/shard_map/mjn,mjk->mkn/dot_general | solution.py:18
  78.0 22.4 %copy.49 = bf16[256,256,128]{2,1,0:T(8,128)(2,1)} copy(bf16[256,256,128]{1,2,0:T(8,128)(2,1)} %convert_bitcast_fusion) | data formatting | bytes 33554432 | tf_op jit(solution)/shard_map/convert_element_type | solution.py:19
  100.4 42.5 %while.56 = (s32[]{:T(128)}, f32[128,256]{1,0:T(8,128)S(1)}, bf16[65536,128]{1,0:T(8,128)(2,1)}, s32[256,256]{1,0:T(8,128)}, s32[]{:T(128)}, /*index=5*/s32[]{:T(128)}, s32[]{:T(128)}, s32[]{:T(128)}, s32[]{:T(128)}, s32[]{:T(128)}) while((s32[]{:T(128)}, f32[128,256]{1,0:T(8,128)S(1)}, bf16[65536,128]{1,0:T(8,128)(2,1)}, ...), condition=%wide.region_8.9_spmd.clone, body=%wide.region_7.8_spmd.clone.sunk | while | flops 539033600 | bytes 6783187 | solution.py:44
  102.6 3.0 %fusion.61 = f32[128,256]{1,0:T(8,128)S(1)} fusion(pred[8192,256]{1,0:T(32,128)(4,1)S(1)} %bitcast_compare_fusion.8, bf16[65536,128]{1,0:T(8,128)(2,1)} %get-tuple-element.577, s32[]{:T(128)S(6)} %select_n.199, f32[128,256]{1,0:T(8,128)S(1)} %get-tuple-element.566, pred[]{:T(512)S(6)} %compare.36), kind=kOutput, calls=%fused_computation.18.clone.1 | convolution fusion | flops 536936448 | bytes 4456453 | tf_op jit(solution)/shard_map/while/body/eval_jaxpr/dot_general | solution.py:38
  107.9 3.0 %fusion.61 = f32[128,256]{1,0:T(8,128)S(1)} fusion(pred[8192,256]{1,0:T(32,128)(4,1)S(1)} %bitcast_compare_fusion.8, bf16[65536,128]{1,0:T(8,128)(2,1)} %get-tuple-element.577, s32[]{:T(128)S(6)} %select_n.199, f32[128,256]{1,0:T(8,128)S(1)} %get-tuple-element.566, pred[]{:T(512)S(6)} %compare.36), kind=kOutput, calls=%fused_computation.18.clone.1 | convolution fusion | flops 536936448 | bytes 4456453 | tf_op jit(solution)/shard_map/while/body/eval_jaxpr/dot_general | solution.py:38
  113.2 3.0 %fusion.61 = f32[128,256]{1,0:T(8,128)S(1)} fusion(pred[8192,256]{1,0:T(32,128)(4,1)S(1)} %bitcast_compare_fusion.8, bf16[65536,128]{1,0:T(8,128)(2,1)} %get-tuple-element.577, s32[]{:T(128)S(6)} %select_n.199, f32[128,256]{1,0:T(8,128)S(1)} %get-tuple-element.566, pred[]{:T(512)S(6)} %compare.36), kind=kOutput, calls=%fused_computation.18.clone.1 | convolution fusion | flops 536936448 | bytes 4456453 | tf_op jit(solution)/shard_map/while/body/eval_jaxpr/dot_general | solution.py:38
  123.9 3.0 %fusion.61 = f32[128,256]{1,0:T(8,128)S(1)} fusion(pred[8192,256]{1,0:T(32,128)(4,1)S(1)} %bitcast_compare_fusion.8, bf16[65536,128]{1,0:T(8,128)(2,1)} %get-tuple-element.577, s32[]{:T(128)S(6)} %select_n.199, f32[128,256]{1,0:T(8,128)S(1)} %get-tuple-element.566, pred[]{:T(512)S(6)} %compare.36), kind=kOutput, calls=%fused_computation.18.clone.1 | convolution fusion | flops 536936448 | bytes 4456453 | tf_op jit(solution)/shard_map/while/body/eval_jaxpr/dot_general | solution.py:38
  129.2 3.0 %fusion.61 = f32[128,256]{1,0:T(8,128)S(1)} fusion(pred[8192,256]{1,0:T(32,128)(4,1)S(1)} %bitcast_compare_fusion.8, bf16[65536,128]{1,0:T(8,128)(2,1)} %get-tuple-element.577, s32[]{:T(128)S(6)} %select_n.199, f32[128,256]{1,0:T(8,128)S(1)} %get-tuple-element.566, pred[]{:T(512)S(6)} %compare.36), kind=kOutput, calls=%fused_computation.18.clone.1 | convolution fusion | flops 536936448 | bytes 4456453 | tf_op jit(solution)/shard_map/while/body/eval_jaxpr/dot_general | solution.py:38
  134.5 3.0 %fusion.61 = f32[128,256]{1,0:T(8,128)S(1)} fusion(pred[8192,256]{1,0:T(32,128)(4,1)S(1)} %bitcast_compare_fusion.8, bf16[65536,128]{1,0:T(8,128)(2,1)} %get-tuple-element.577, s32[]{:T(128)S(6)} %select_n.199, f32[128,256]{1,0:T(8,128)S(1)} %get-tuple-element.566, pred[]{:T(512)S(6)} %compare.36), kind=kOutput, calls=%fused_computation.18.clone.1 | convolution fusion | flops 536936448 | bytes 4456453 | tf_op jit(solution)/shard_map/while/body/eval_jaxpr/dot_general | solution.py:38
  144.4 8.1 %convert_bitcast_fusion.1 = bf16[256,256,128]{1,2,0:T(8,128)(2,1)} fusion(bf16[256,2048]{0,1:T(8,128)(2,1)S(1)} %copy.46, bf16[128,2048]{0,1:T(8,128)(2,1)S(1)} %copy.45), kind=kOutput, calls=%fused_computation.23 | convolution fusion | flops 142606336 | bytes 18350080 | tf_op jit(solution)/shard_map/mjn,mjk->mkn/dot_general | solution.py:18
  152.5 22.4 %copy.47 = bf16[256,256,128]{2,1,0:T(8,128)(2,1)} copy(bf16[256,256,128]{1,2,0:T(8,128)(2,1)} %convert_bitcast_fusion.1) | data formatting | bytes 33554432 | tf_op jit(solution)/shard_map/convert_element_type | solution.py:19
  174.9 42.5 %while.55 = (s32[]{:T(128)}, f32[128,256]{1,0:T(8,128)S(1)}, bf16[65536,128]{1,0:T(8,128)(2,1)}, s32[256,256]{1,0:T(8,128)}, s32[]{:T(128)}, /*index=5*/s32[]{:T(128)}, s32[]{:T(128)}, s32[]{:T(128)}, s32[]{:T(128)}, s32[]{:T(128)}) while((s32[]{:T(128)}, f32[128,256]{1,0:T(8,128)S(1)}, bf16[65536,128]{1,0:T(8,128)(2,1)}, ...), condition=%wide.region_6.7_spmd.clone, body=%wide.region_5.6_spmd.clone.sunk | while | flops 539033600 | bytes 6783187 | solution.py:44
  177.1 3.0 %fusion.58 = f32[128,256]{1,0:T(8,128)S(1)} fusion(pred[8192,256]{1,0:T(32,128)(4,1)S(1)} %bitcast_compare_fusion.7, bf16[65536,128]{1,0:T(8,128)(2,1)} %get-tuple-element.607, s32[]{:T(128)S(6)} %select_n.197, f32[128,256]{1,0:T(8,128)S(1)} %get-tuple-element.596, pred[]{:T(512)S(6)} %compare.35), kind=kOutput, calls=%fused_computation.11.clone.1 | convolution fusion | flops 536936448 | bytes 4456453 | tf_op jit(solution)/shard_map/while/body/eval_jaxpr/dot_general | solution.py:38
  182.4 3.0 %fusion.58 = f32[128,256]{1,0:T(8,128)S(1)} fusion(pred[8192,256]{1,0:T(32,128)(4,1)S(1)} %bitcast_compare_fusion.7, bf16[65536,128]{1,0:T(8,128)(2,1)} %get-tuple-element.607, s32[]{:T(128)S(6)} %select_n.197, f32[128,256]{1,0:T(8,128)S(1)} %get-tuple-element.596, pred[]{:T(512)S(6)} %compare.35), kind=kOutput, calls=%fused_computation.11.clone.1 | convolution fusion | flops 536936448 | bytes 4456453 | tf_op jit(solution)/shard_map/while/body/eval_jaxpr/dot_general | solution.py:38
  187.8 3.0 %fusion.58 = f32[128,256]{1,0:T(8,128)S(1)} fusion(pred[8192,256]{1,0:T(32,128)(4,1)S(1)} %bitcast_compare_fusion.7, bf16[65536,128]{1,0:T(8,128)(2,1)} %get-tuple-element.607, s32[]{:T(128)S(6)} %select_n.197, f32[128,256]{1,0:T(8,128)S(1)} %get-tuple-element.596, pred[]{:T(512)S(6)} %compare.35), kind=kOutput, calls=%fused_computation.11.clone.1 | convolution fusion | flops 536936448 | bytes 4456453 | tf_op jit(solution)/shard_map/while/body/eval_jaxpr/dot_general | solution.py:38
  193.1 3.0 %fusion.58 = f32[128,256]{1,0:T(8,128)S(1)} fusion(pred[8192,256]{1,0:T(32,128)(4,1)S(1)} %bitcast_compare_fusion.7, bf16[65536,128]{1,0:T(8,128)(2,1)} %get-tuple-element.607, s32[]{:T(128)S(6)} %select_n.197, f32[128,256]{1,0:T(8,128)S(1)} %get-tuple-element.596, pred[]{:T(512)S(6)} %compare.35), kind=kOutput, calls=%fused_computation.11.clone.1 | convolution fusion | flops 536936448 | bytes 4456453 | tf_op jit(solution)/shard_map/while/body/eval_jaxpr/dot_general | solution.py:38
  198.4 3.0 %fusion.58 = f32[128,256]{1,0:T(8,128)S(1)} fusion(pred[8192,256]{1,0:T(32,128)(4,1)S(1)} %bitcast_compare_fusion.7, bf16[65536,128]{1,0:T(8,128)(2,1)} %get-tuple-element.607, s32[]{:T(128)S(6)} %select_n.197, f32[128,256]{1,0:T(8,128)S(1)} %get-tuple-element.596, pred[]{:T(512)S(6)} %compare.35), kind=kOutput, calls=%fused_computation.11.clone.1 | convolution fusion | flops 536936448 | bytes 4456453 | tf_op jit(solution)/shard_map/while/body/eval_jaxpr/dot_general | solution.py:38
  209.0 3.0 %fusion.58 = f32[128,256]{1,0:T(8,128)S(1)} fusion(pred[8192,256]{1,0:T(32,128)(4,1)S(1)} %bitcast_compare_fusion.7, bf16[65536,128]{1,0:T(8,128)(2,1)} %get-tuple-element.607, s32[]{:T(128)S(6)} %select_n.197, f32[128,256]{1,0:T(8,128)S(1)} %get-tuple-element.596, pred[]{:T(512)S(6)} %compare.35), kind=kOutput, calls=%fused_computation.11.clone.1 | convolution fusion | flops 536936448 | bytes 4456453 | tf_op jit(solution)/shard_map/while/body/eval_jaxpr/dot_general | solution.py:38
  214.3 3.0 %fusion.58 = f32[128,256]{1,0:T(8,128)S(1)} fusion(pred[8192,256]{1,0:T(32,128)(4,1)S(1)} %bitcast_compare_fusion.7, bf16[65536,128]{1,0:T(8,128)(2,1)} %get-tuple-element.607, s32[]{:T(128)S(6)} %select_n.197, f32[128,256]{1,0:T(8,128)S(1)} %get-tuple-element.596, pred[]{:T(512)S(6)} %compare.35), kind=kOutput, calls=%fused_computation.11.clone.1 | convolution fusion | flops 536936448 | bytes 4456453 | tf_op jit(solution)/shard_map/while/body/eval_jaxpr/dot_general | solution.py:38
  218.2 12.2 %all-to-all-start.1 = ((f32[2,32,4,256]{3,2,0,1:T(4,128)}), f32[2,32,4,256]{3,2,0,1:T(4,128)S(1)}, u32[]{:S(2)}, u32[]{:S(2)}) async-start(f32[2,32,4,256]{3,2,0,1:T(4,128)} %pad_maximum_fusion), calls=%async_computation.1 | async-start | bytes 524288 | tf_op jit(solution)/shard_map/all_to_all | solution.py:120
  230.5 8.9 %all-to-all-done.1 = f32[2,32,4,256]{3,2,0,1:T(4,128)S(1)} async-done(((f32[2,32,4,256]{3,2,0,1:T(4,128)}), f32[2,32,4,256]{3,2,0,1:T(4,128)S(1)}, u32[]{:S(2)}, u32[]{:S(2)}) %all-to-all-start.1) | async-done | bytes 262176 | tf_op jit(solution)/shard_map/all_to_all | solution.py:120
  (144 shorter events, 83.6 us)
Async XLA Ops:
  0.6 14.8 %copy-start = (bf16[256,64]{0,1:T(8,128)(2,1)S(1)}, bf16[256,64]{0,1:T(8,128)(2,1)}, u32[]{:S(2)}) copy-start(bf16[256,64]{0,1:T(8,128)(2,1)} %param.16) | copy-start | bytes 98308
  6.1 62.1 %all-to-all-start = ((bf16[2,32,4,2048]{3,2,0,1:T(4,128)(2,1)}), bf16[2,32,4,2048]{3,2,0,1:T(4,128)(2,1)S(1)}, u32[]{:S(2)}, u32[]{:S(2)}) async-start(bf16[2,32,4,2048]{3,2,0,1:T(4,128)(2,1)} %copy.44), calls=%async_computation | async-start | bytes 2097152 | tf_op jit(solution)/shard_map/all_to_all | solution.py:103
  63.8 1.6 copy-start.3
  63.8 3.4 %copy-start.2 = (s32[2,256,256]{2,1,0:T(8,128)S(1)}, s32[2,256,256]{2,1,0:T(8,128)}, u32[]{:S(2)}) copy-start(s32[2,256,256]{2,1,0:T(8,128)} %param.17) | copy-start | bytes 1572868
  217.4 23.5 %copy-start.1 = (bf16[256,64]{0,1:T(8,128)(2,1)S(1)}, bf16[256,64]{0,1:T(8,128)(2,1)}, u32[]{:S(2)}) copy-start(bf16[256,64]{0,1:T(8,128)(2,1)} %param.16) | copy-start | bytes 98308
  218.2 21.1 %all-to-all-start.1 = ((f32[2,32,4,256]{3,2,0,1:T(4,128)}), f32[2,32,4,256]{3,2,0,1:T(4,128)S(1)}, u32[]{:S(2)}, u32[]{:S(2)}) async-start(f32[2,32,4,256]{3,2,0,1:T(4,128)} %pad_maximum_fusion), calls=%async_computation.1 | async-start | bytes 524288 | tf_op jit(solution)/shard_map/all_to_all | solution.py:120
where the time goes:
time: 244 us; the launch traced here: 241 us
  local copies, waits for them, and re-layouts  77.3 us (32%)
  matrix products  75.9 us (31%)
  other arithmetic  31 us (13%)
  blocking collectives  24.2 us (10%)
  starting transfers between devices  20.8 us (9%)
  waiting for transfers between devices  8.87 us (4%)
    dot_general x20, matrix products, one_step(): lax.dot_general(part_tables, onehot, (((0,), (0,)), ((), ())), preferred_...  58.1 us
    convert_element_type x2, local copies, waits for them, and re-layouts, build_tables(): tables.astype(jnp.bfloat16).reshape(subspaces * centers, vector_count)  44.7 us
    eq x20, other arithmetic, one_step(): code_block[:, None, :] == levels[None, :, None]  28.3 us
    all_gather x1, blocking collectives, body(): coarse_tables = lax.all_gather(own_tables, 'group', axis=1, tiled=True)  24.2 us
    dot_general x3, matrix products, build_tables(): jnp.einsum('mjn,mjk->mkn', pieces, entries, preferred_element_type=jnp.fl...  16.5 us
    dynamic_slice x16, local copies, waits for them, and re-layouts, one_step(): lax.dynamic_slice_in_dim(code_rows, step_index * group_size, group_size, 0)  12.2 us
    all_to_all x1, starting transfers between devices, body(): lax.all_to_all(computed, 'shard', split_axis=1, concat_axis=1, tiled=True)  12.2 us
    all_to_all x1, waiting for transfers between devices, body(): lax.all_to_all(computed, 'shard', split_axis=1, concat_axis=1, tiled=True)  8.87 us
  transfers between devices with their start and end apart: 2, of which 1 were waited for; matrix products, arithmetic and copies ran while one was open for 12% of the time, Pallas kernels for 0%

commit v1 on v0

v1 whole, which is shorter than its diff:
```python
import functools

import jax
import jax.numpy as jnp
from jax import lax
from jax.experimental import pallas as pl
from jax.experimental.pallas import tpu as pltpu
from jax.sharding import PartitionSpec as P

PREFIX = 64
BLOCK = 128
CAPACITY = 4
CHUNK = 64
SPAN = 512
LANES = 128


def picked(low_half, high_half, code):
    within = code & (LANES - 1)
    from_low = jnp.take_along_axis(low_half, within, axis=1)
    from_high = jnp.take_along_axis(high_half, within, axis=1)
    return jnp.where(code < LANES, from_low, from_high)


def rebuild_pair(table, codes, first, base):
    parts = []
    for u in range(2):
        low_half = table[pl.ds(base + u * 8, 8), :LANES]
        high_half = table[pl.ds(base + u * 8, 8), LANES:]
        code = codes[first + u : first + u + 1]
        spans = []
        for r in range(0, codes.shape[1], LANES):
            index = jnp.broadcast_to(code[:, r : r + LANES], (8, LANES))
            spans.append(picked(low_half, high_half, index))
        parts.append(jnp.concatenate(spans, axis=1))
    return jnp.concatenate(parts, axis=0).astype(jnp.bfloat16)


def route_kernel(shortlist_ref, owner_ref, queries_ref, out_ref):
    lists = shortlist_ref[...]
    probes, count = lists.shape
    clusters = owner_ref.shape[1]
    ids = lax.broadcasted_iota(jnp.int32, (clusters, count), 0)
    named = jnp.zeros((clusters, count), jnp.float32)
    for entry in range(probes):
        named += (lists[entry : entry + 1, :] == ids).astype(jnp.float32)
    row = lax.broadcasted_iota(jnp.int32, (count, count), 0)
    col = lax.broadcasted_iota(jnp.int32, (count, count), 1)
    rank = jnp.dot(named, (row < col).astype(jnp.float32), preferred_element_type=jnp.float32)
    places = clusters * CAPACITY
    place = lax.broadcasted_iota(jnp.int32, (places, clusters), 0)
    stored = (owner_ref[...] == place // CAPACITY).astype(jnp.float32)
    named_at = jnp.dot(stored, named, preferred_element_type=jnp.float32)
    rank_at = jnp.dot(stored, rank, preferred_element_type=jnp.float32)
    turn = (lax.broadcasted_iota(jnp.int32, (places, count), 0) % CAPACITY).astype(jnp.float32)
    routing = jnp.where(rank_at == turn, named_at, 0.0).astype(jnp.bfloat16)
    out_ref[...] = jnp.dot(
        routing, queries_ref[...], preferred_element_type=jnp.float32
    ).astype(jnp.bfloat16)


def rebuild_kernel(codes_ref, codebook_ref, out_ref, table):
    table[...] = codebook_ref[...].astype(jnp.float32).T
    for local_id in range(codes_ref.shape[0]):

        def step(index, carry, local_id=local_id):
            first = pl.multiple_of(index * 8, 8)
            codes = codes_ref[local_id, pl.ds(first, 8), :]
            for pair in range(4):
                base = pl.multiple_of(first * 8 + pair * 16, 16)
                out_ref[local_id, pl.ds(base, 16), :] = rebuild_pair(table, codes, pair * 2, base)
            return carry

        lax.fori_loop(0, codes_ref.shape[1] // 8, step, 0, unroll=8)


def coarse_kernel(prefix_ref, codes_ref, codebook_ref, out_ref, table):
    @pl.when(pl.program_id(0) == 0)
    def _():
        table[...] = codebook_ref[...].astype(jnp.float32)

    codes = codes_ref[...]
    rebuilt = jnp.concatenate(
        [rebuild_pair(table, codes, first, first * 8) for first in range(0, codes.shape[0], 2)],
        axis=0,
    )
    out_ref[...] = jnp.dot(prefix_ref[...], rebuilt, preferred_element_type=jnp.float32)


def score_kernel(counts_ref, items_ref, rebuilt_ref, out_ref):
    local_count = rebuilt_ref.shape[0]
    rows = rebuilt_ref.shape[2]
    shape = (items_ref.shape[0], rows)
    turn = lax.broadcasted_iota(jnp.int32, shape, 0) // CAPACITY % local_count
    row_ids = lax.broadcasted_iota(jnp.int32, shape, 1)
    total = jnp.zeros(shape, jnp.float32)
    for local_id in range(local_count):
        scores = jnp.dot(
            items_ref[...], rebuilt_ref[local_id], preferred_element_type=jnp.float32
        )
        kept = (turn == local_id) & (row_ids < BLOCK * counts_ref[local_id])
        total = jnp.where(kept, scores, total)
    out_ref[...] = total


def gathered(block, axis):
    size = lax.axis_size(axis)
    place = lax.axis_index(axis)
    step = 1
    while step < size:
        other = lax.ppermute(block, axis, [(i, i ^ step) for i in range(size)])
        later = place & step != 0
        block = jnp.concatenate(
            [jnp.where(later, other, block), jnp.where(later, block, other)], axis=0
        )
        step *= 2
    return block


def body(
    queries,
    fine_codebook,
    coarse_codebook,
    fine_codes,
    coarse_codes,
    shortlist,
    owner,
    block_counts,
):
    shards = lax.axis_size("shard")
    groups = lax.axis_size("group")
    local_count, subspaces, row_count = fine_codes.shape
    per_device, width = queries.shape[1:]
    probes = shortlist.shape[2]
    clusters = owner.shape[0]
    centers = fine_codebook.shape[0]
    slab_subspaces, slab_rows = coarse_codes.shape
    positions = clusters * CAPACITY
    queries = queries[0]
    lists = shortlist[0]

    outgoing = pl.pallas_call(
        route_kernel,
        out_shape=jax.ShapeDtypeStruct((positions, width), jnp.bfloat16),
        name="route",
    )(lists.T, owner.reshape(1, clusters), queries)
    arrived = lax.all_to_all(
        outgoing.reshape(shards, positions // shards, width), "shard", 0, 0, tiled=True
    )

    prefixes = gathered(queries[:, :PREFIX], "group")

    rebuilt = pl.pallas_call(
        rebuild_kernel,
        grid=(subspaces // CHUNK,),
        in_specs=[
            pl.BlockSpec((local_count, CHUNK, row_count), lambda i: (0, i, 0)),
            pl.BlockSpec((centers, CHUNK * 8), lambda i: (0, i)),
        ],
        out_specs=pl.BlockSpec((local_count, CHUNK * 8, row_count), lambda i: (0, i, 0)),
        out_shape=jax.ShapeDtypeStruct((local_count, width, row_count), jnp.bfloat16),
        scratch_shapes=[pltpu.VMEM((CHUNK * 8, centers), jnp.float32)],
        cost_estimate=pl.CostEstimate(
            flops=4_000_000_000, bytes_accessed=4_000_000, transcendentals=0
        ),
        name="rebuild",
    )(fine_codes, fine_codebook)

    coarse_scores = pl.pallas_call(
        coarse_kernel,
        grid=(slab_rows // SPAN,),
        in_specs=[
            pl.BlockSpec((groups * per_device, PREFIX), lambda i: (0, 0)),
            pl.BlockSpec((slab_subspaces, SPAN), lambda i: (0, i)),
            pl.BlockSpec((PREFIX, centers), lambda i: (0, 0)),
        ],
        out_specs=pl.BlockSpec((groups * per_device, SPAN), lambda i: (0, i)),
        out_shape=jax.ShapeDtypeStruct((groups * per_device, slab_rows), jnp.float32),
        scratch_shapes=[pltpu.VMEM((PREFIX, centers), jnp.float32)],
        cost_estimate=pl.CostEstimate(
            flops=2_000_000_000, bytes_accessed=4_000_000, transcendentals=0
        ),
        name="coarse",
    )(prefixes, coarse_codes, coarse_codebook.T)

    computed = pl.pallas_call(
        score_kernel,
        in_specs=[
            pl.BlockSpec(memory_space=pltpu.SMEM),
            pl.BlockSpec(memory_space=pltpu.VMEM),
            pl.BlockSpec(memory_space=pltpu.VMEM),
        ],
        out_shape=jax.ShapeDtypeStruct((positions, row_count), jnp.float32),
        name="score",
    )(block_counts, arrived.reshape(positions, width), rebuilt)
    returned = lax.all_to_all(
        computed.reshape(shards, positions // shards, row_count), "shard", 0, 0, tiled=True
    ).reshape(positions, row_count)

    flat = lists.reshape(-1)
    storage = jnp.sum(
        jnp.where(flat[:, None] == jnp.arange(clusters)[None, :], owner[None, :], 0), axis=1
    )
    items = jnp.arange(flat.shape[0])
    earlier = (flat[:, None] == flat[None, :]) & (items[:, None] > items[None, :])
    target = storage * CAPACITY + jnp.sum(earlier.astype(jnp.int32), axis=1)
    fine_scores = jnp.take(returned, target, axis=0)
    return (
        coarse_scores.reshape(groups, per_device, slab_rows),
        fine_scores.reshape(1, per_device, probes, row_count),
    )


def solution(mesh):
    in_specs = (
        P("group", "shard", None),
        P(),
        P(),
        P("shard", None, None),
        P(None, "group"),
        P("group", "shard", None),
        P(),
        P("shard"),
    )
    out_specs = (P(None, "shard", "group"), P("group", "shard", None, None))
    return jax.shard_map(body, mesh=mesh, in_specs=in_specs, out_specs=out_specs, check_vma=False)
```

time: 244 us -> 57.2 us (0.23)
  matrix products: 75.9 us -> 0 us
  local copies, waits for them, and re-layouts: 77.3 us -> 2.66 us
  other arithmetic: 31 us -> 2.39 us
  blocking collectives: 24.2 us -> 0 us
  Pallas kernels: 0 us -> 17.3 us
  starting transfers between devices: 20.8 us -> 28.3 us
  waiting for transfers between devices: 8.87 us -> 4.92 us
    dot_general x24 -> x0, matrix products: 75.9 us -> none  [the longest x20 58.1 us: one_step(): lax.dot_general(part_tables, onehot, (((0,), (0,)), ((), ())), preferred_...]
    convert_element_type x2 -> x0, local copies, waits for them, and re-layouts: 44.7 us -> none  [build_tables(): tables.astype(jnp.bfloat16).reshape(subspaces * centers, vector_count)]
    eq x20 -> x0, other arithmetic: 28.3 us -> none  [one_step(): code_block[:, None, :] == levels[None, :, None]]
    all_gather x1 -> x0, blocking collectives: 24.2 us -> none  [body(): coarse_tables = lax.all_gather(own_tables, 'group', axis=1, tiled=True)]
    pallas_call x0 -> x4, Pallas kernels: none -> 17.3 us  [the longest x1 5.78 us: body(): pl.pallas_call(rebuild_kernel, grid=(subspaces // CHUNK,), in_specs=[pl.B...]
    dynamic_slice x20 -> x0, local copies, waits for them, and re-layouts: 15.3 us -> none  [the longest x16 12.2 us: one_step(): lax.dynamic_slice_in_dim(code_rows, step_index * group_size, group_size, 0)]
    ppermute x0 -> x3, starting transfers between devices: none -> 11.1 us  [gathered(): other = lax.ppermute(block, axis, [(i, i ^ step) for i in range(size)])]
    all_to_all x2, waiting for transfers between devices: 8.87 us -> 2.57 us  [the longest x1 2.57 us: body(): lax.all_to_all(computed.reshape(shards, positions // shards, row_count),...]
  transfers between devices with their start and end apart: 2 -> 5, of which waited for: 1 -> 3; matrix products, arithmetic and copies ran while one was open for 12% -> 3% of each run, Pallas kernels for 0% -> 25%
where the time goes in v1:
time: 57.2 us; the launch traced here: 56.3 us
  starting transfers between devices  28.3 us (49%)
  Pallas kernels  17.3 us (30%)
  waiting for transfers between devices  4.92 us (9%)
  local copies, waits for them, and re-layouts  2.66 us (5%)
  other arithmetic  2.39 us (4%)
  between operations  0.74 us (1%)
    ppermute x3, starting transfers between devices, gathered(): other = lax.ppermute(block, axis, [(i, i ^ step) for i in range(size)])  11.1 us
    all_to_all x1, starting transfers between devices, body(): lax.all_to_all(computed.reshape(shards, positions // shards, row_count),...  9.11 us
    all_to_all x1, starting transfers between devices, body(): lax.all_to_all(outgoing.reshape(shards, positions // shards, width), 'sha...  8.04 us
    pallas_call x1, Pallas kernels, body(): pl.pallas_call(rebuild_kernel, grid=(subspaces // CHUNK,), in_specs=[pl.B...  5.78 us
    pallas_call x1, Pallas kernels, body(): pl.pallas_call(coarse_kernel, grid=(slab_rows // SPAN,), in_specs=[pl.Blo...  5.71 us
    pallas_call x1, Pallas kernels, body(): pl.pallas_call(score_kernel, in_specs=[pl.BlockSpec(memory_space=pltpu.SM...  3.35 us
    all_to_all x1, waiting for transfers between devices, body(): lax.all_to_all(computed.reshape(shards, positions // shards, row_count),...  2.57 us
    pallas_call x1, Pallas kernels, body(): pl.pallas_call(route_kernel, out_shape=jax.ShapeDtypeStruct((positions, w...  2.5 us
  transfers between devices with their start and end apart: 5, of which 3 were waited for; matrix products, arithmetic and copies ran while one was open for 3% of the time, Pallas kernels for 25%

profile of v1, /device:TPU:1, one launch (start us, length us, event | category | flops | bytes accessed | tf_op | source)
XLA Modules:
  0.0 56.3 jit_solution(11048527795782022504)
XLA Ops:
  0.6 0.0 copy-start.1
  0.7 0.7 %slice.6 = bf16[16,64]{1,0:T(8,128)(2,1)S(1)} slice(bf16[16,2048]{1,0:T(8,128)(2,1)} %bitcast.21), slice={[0:16], [0:64]} | slice | bytes 4096 | tf_op jit(solution)/shard_map/slice | solution.py:151
  1.4 2.5 %collective-permute-start = (bf16[16,64]{1,0:T(8,128)(2,1)S(1)}, bf16[16,64]{1,0:T(8,128)(2,1)S(1)}, u32[]{:S(2)}, u32[]{:S(2)}) collective-permute-start(bf16[16,64]{1,0:T(8,128)(2,1)S(1)} %slice.6), channel_id=1, source_target_pairs={{0,32},{32,0},{64,96},{96,64},{128,160},{160,128},{192,224},{224,1... | collective-permute-start | bytes 6152 | tf_op jit(solution)/shard_map/ppermute | solution.py:111
  3.8 2.5 %route.1 = bf16[256,2048]{1,0:T(8,128)(2,1)} custom-call(s32[8,16]{1,0:T(8,128)} %bitcast.24, s32[1,64]{1,0:T(1,128)} %bitcast.25, bf16[16,2048]{1,0:T(8,128)(2,1)} %bitcast.22), custom_call_target="tpu_custom_call" | custom-call | tf_op jit(solution)/shard_map/route/pallas_call | solution.py:142
  6.3 8.0 %all-to-all-start = ((bf16[32,8,2048]{2,1,0:T(8,128)(2,1)}), bf16[32,8,2048]{2,1,0:T(8,128)(2,1)S(1)}, u32[]{:S(2)}, u32[]{:S(2)}) async-start(bf16[32,8,2048]{2,1,0:T(8,128)(2,1)} %bitcast.19), calls=%async_computation | async-start | bytes 2097152 | tf_op jit(solution)/shard_map/all_to_all | solution.py:147
  14.4 0.1 copy.12
  14.4 0.1 eq.28
  14.5 0.2 convert_reduce_fusion
  14.7 0.1 select_reduce_fusion
  14.8 5.8 %rebuild.1.rebuilt_ref = bf16[2,2048,256]{2,1,0:T(8,128)(2,1)} custom-call(s32[2,256,256]{2,1,0:T(8,128)} %codes_ref.3, bf16[256,2048]{1,0:T(8,128)(2,1)} %codebook_ref.1), custom_call_target="tpu_custom_call" | custom-call | flops 4000000000 | bytes 4000000 | tf_op jit(solution)/shard_map/rebuild/pallas_call | solution.py:153
  20.6 0.1 add.42
  20.7 0.7 %broadcast_select_fusion.5 = (bf16[16,64]{1,0:T(8,128)(2,1)S(1)}, bf16[16,64]{1,0:T(8,128)(2,1)S(1)}) fusion(bf16[16,64]{1,0:T(8,128)(2,1)S(1)} %collective-permute-done, pred[]{:T(512)S(6)} %ne.11, bf16[16,2048]{1,0:T(8,128)(2,1)} %bitcast.23), kind=kLoop, calls=%fused_computation.18 | loop fusion | flops 2048 | bytes 8193 | tf_op jit(solution)/shard_map/jit(_where)/select_n | solution.py:114
  21.4 3.1 %collective-permute-start.1 = (bf16[32,64]{1,0:T(8,128)(2,1)S(1)}, bf16[32,64]{1,0:T(8,128)(2,1)S(1)}, u32[]{:S(2)}, u32[]{:S(2)}) collective-permute-start(bf16[32,64]{1,0:T(8,128)(2,1)S(1)} %pad_maximum_fusion.2), channel_id=1, source_target_pairs={{0,64},{32,96},{64,0},{96,32},{128,192},{160,224},{192,128},{224,1... | collective-permute-start | bytes 12296 | tf_op jit(solution)/shard_map/ppermute | solution.py:111
  24.5 1.2 %collective-permute-done.1 = bf16[32,64]{1,0:T(8,128)(2,1)S(1)} collective-permute-done((bf16[32,64]{1,0:T(8,128)(2,1)S(1)}, bf16[32,64]{1,0:T(8,128)(2,1)S(1)}, u32[]{:S(2)}, u32[]{:S(2)}) %collective-permute-start.1) | collective-permute-done | bytes 4128 | tf_op jit(solution)/shard_map/ppermute | solution.py:111
  25.7 5.6 %collective-permute-start.2 = (bf16[64,64]{1,0:T(8,128)(2,1)S(1)}, bf16[64,64]{1,0:T(8,128)(2,1)S(1)}, u32[]{:S(2)}, u32[]{:S(2)}) collective-permute-start(bf16[64,64]{1,0:T(8,128)(2,1)S(1)} %pad_maximum_fusion.1), channel_id=1, source_target_pairs={{0,128},{32,160},{64,192},{96,224},{128,0},{160,32},{192,64},{224,... | collective-permute-start | bytes 24584 | tf_op jit(solution)/shard_map/ppermute | solution.py:111
  31.3 1.1 %collective-permute-done.2 = bf16[64,64]{1,0:T(8,128)(2,1)S(1)} collective-permute-done((bf16[64,64]{1,0:T(8,128)(2,1)S(1)}, bf16[64,64]{1,0:T(8,128)(2,1)S(1)}, u32[]{:S(2)}, u32[]{:S(2)}) %collective-permute-start.2) | collective-permute-done | bytes 8224 | tf_op jit(solution)/shard_map/ppermute | solution.py:111
  32.5 1.0 %copy-done = bf16[32,8,2048]{2,1,0:T(8,128)(2,1)} copy-done((bf16[32,8,2048]{2,1,0:T(8,128)(2,1)}, bf16[32,8,2048]{2,1,0:T(8,128)(2,1)S(1)}, u32[]{:S(2)}) %copy-start) | copy-done | bytes 1048600
  33.4 3.4 %score.1 = f32[256,256]{1,0:T(8,128)} custom-call(s32[2]{0:T(128)} %counts_ref.1, bf16[256,2048]{1,0:T(8,128)(2,1)} %bitcast.18, bf16[2,2048,256]{2,1,0:T(8,128)(2,1)} %rebuild.1.rebuilt_ref), custom_call_target="tpu_custom_call" | custom-call | tf_op jit(solution)/shard_map/score/pallas_call | solution.py:186
  36.8 9.1 %all-to-all-start.1 = ((f32[32,8,256]{2,1,0:T(8,128)}), f32[32,8,256]{2,1,0:T(8,128)S(1)}, u32[]{:S(2)}, u32[]{:S(2)}) async-start(f32[32,8,256]{2,1,0:T(8,128)} %bitcast.20), calls=%async_computation.1 | async-start | bytes 524288 | tf_op jit(solution)/shard_map/all_to_all | solution.py:196
  45.9 0.6 %pad_maximum_fusion.prefix_ref = bf16[128,64]{1,0:T(8,128)(2,1)} fusion(bf16[64,64]{1,0:T(8,128)(2,1)S(1)} %get-tuple-element.7, bf16[64,64]{1,0:T(8,128)(2,1)S(1)} %get-tuple-element.6), kind=kLoop, calls=%fused_computation.5 | loop fusion | flops 32768 | bytes 32768 | tf_op jit(solution)/shard_map/concatenate | solution.py:113
  46.5 5.7 %coarse.1 = f32[128,4096]{1,0:T(8,128)} custom-call(bf16[128,64]{1,0:T(8,128)(2,1)} %pad_maximum_fusion.prefix_ref, s32[8,4096]{1,0:T(8,128)} %codes_ref.2, bf16[64,256]{1,0:T(8,128)(2,1)} %bitcast.26), custom_call_target="tpu_custom_call" | custom-call | flops 2000000000 | bytes 4000000 | tf_op jit(solution)/shard_map/coarse/pallas_call | solution.py:169
  52.2 2.6 %all-to-all-done.1 = f32[32,8,256]{2,1,0:T(8,128)S(1)} async-done(((f32[32,8,256]{2,1,0:T(8,128)}), f32[32,8,256]{2,1,0:T(8,128)S(1)}, u32[]{:S(2)}, u32[]{:S(2)}) %all-to-all-start.1) | async-done | bytes 262176 | tf_op jit(solution)/shard_map/all_to_all | solution.py:196
  54.8 0.8 %gather_fusion = f32[128,256]{1,0:T(8,128)S(1)} fusion(f32[256,256]{1,0:T(8,128)S(1)} %bitcast.17, s32[1024]{0:T(1024)S(1)} %pad_clamp_fusion), kind=kCustom, calls=%fused_computation | custom fusion | bytes 262656 | tf_op jit(solution)/shard_map/jit(_take)/gather | solution.py:207
  55.5 0.7 %bitcast_select_fusion = f32[1,16,8,256]{3,2,1,0:T(8,128)} fusion(f32[128,256]{1,0:T(8,128)S(1)} %gather_fusion, pred[16,8]{1,0:T(8,128)(4,1)S(1)} %compare_and_fusion), kind=kLoop, calls=%fused_computation.1 | loop fusion | flops 32768 | bytes 262272 | tf_op jit(solution)/shard_map/jit(_take)/select_n | solution.py:207
  (13 shorter events, 0.1 us)
Async XLA Ops:
  0.6 13.7 %copy-start.1 = (s32[1,16,8]{1,2,0:T(8,128)S(1)}, s32[1,16,8]{1,2,0:T(8,128)}, u32[]{:S(2)}) copy-start(s32[1,16,8]{1,2,0:T(8,128)} %param.13) | copy-start | bytes 1540
  0.6 14.1 %copy-start.2 = (s32[64]{0:T(128)S(1)}, s32[64]{0:T(128)}, u32[]{:S(2)}) copy-start(s32[64]{0:T(128)} %param.14) | copy-start | bytes 772
  1.4 19.3 %collective-permute-start = (bf16[16,64]{1,0:T(8,128)(2,1)S(1)}, bf16[16,64]{1,0:T(8,128)(2,1)S(1)}, u32[]{:S(2)}, u32[]{:S(2)}) collective-permute-start(bf16[16,64]{1,0:T(8,128)(2,1)S(1)} %slice.6), channel_id=1, source_target_pairs={{0,32},{32,0},{64,96},{96,64},{128,160},{160,128},{192,224},{224,1... | collective-permute-start | bytes 6152 | tf_op jit(solution)/shard_map/ppermute | solution.py:111
  6.3 26.1 %all-to-all-start = ((bf16[32,8,2048]{2,1,0:T(8,128)(2,1)}), bf16[32,8,2048]{2,1,0:T(8,128)(2,1)S(1)}, u32[]{:S(2)}, u32[]{:S(2)}) async-start(bf16[32,8,2048]{2,1,0:T(8,128)(2,1)} %bitcast.19), calls=%async_computation | async-start | bytes 2097152 | tf_op jit(solution)/shard_map/all_to_all | solution.py:147
  21.4 4.3 %collective-permute-start.1 = (bf16[32,64]{1,0:T(8,128)(2,1)S(1)}, bf16[32,64]{1,0:T(8,128)(2,1)S(1)}, u32[]{:S(2)}, u32[]{:S(2)}) collective-permute-start(bf16[32,64]{1,0:T(8,128)(2,1)S(1)} %pad_maximum_fusion.2), channel_id=1, source_target_pairs={{0,64},{32,96},{64,0},{96,32},{128,192},{160,224},{192,128},{224,1... | collective-permute-start | bytes 12296 | tf_op jit(solution)/shard_map/ppermute | solution.py:111
  25.7 6.7 %collective-permute-start.2 = (bf16[64,64]{1,0:T(8,128)(2,1)S(1)}, bf16[64,64]{1,0:T(8,128)(2,1)S(1)}, u32[]{:S(2)}, u32[]{:S(2)}) collective-permute-start(bf16[64,64]{1,0:T(8,128)(2,1)S(1)} %pad_maximum_fusion.1), channel_id=1, source_target_pairs={{0,128},{32,160},{64,192},{96,224},{128,0},{160,32},{192,64},{224,... | collective-permute-start | bytes 24584 | tf_op jit(solution)/shard_map/ppermute | solution.py:111
  32.5 1.0 %copy-start = (bf16[32,8,2048]{2,1,0:T(8,128)(2,1)}, bf16[32,8,2048]{2,1,0:T(8,128)(2,1)S(1)}, u32[]{:S(2)}) copy-start(bf16[32,8,2048]{2,1,0:T(8,128)(2,1)S(1)} %all-to-all-done) | copy-start | bytes 3145732
  36.8 18.0 %all-to-all-start.1 = ((f32[32,8,256]{2,1,0:T(8,128)}), f32[32,8,256]{2,1,0:T(8,128)S(1)}, u32[]{:S(2)}, u32[]{:S(2)}) async-start(f32[32,8,256]{2,1,0:T(8,128)} %bitcast.20), calls=%async_computation.1 | async-start | bytes 524288 | tf_op jit(solution)/shard_map/all_to_all | solution.py:196

commit v2 on v1

v2 whole, which is shorter than its diff:
```python
import functools

import jax
import jax.numpy as jnp
from jax import lax
from jax.experimental import pallas as pl
from jax.experimental.pallas import tpu as pltpu
from jax.sharding import PartitionSpec as P

PREFIX = 64
BLOCK = 128
CAPACITY = 4
CHUNK = 64
SPAN = 2048
LANES = 128


def looked_up(halves, code):
    within = code & (LANES - 1)
    low = code < LANES
    found = [
        (jnp.take_along_axis(first, within, axis=1), jnp.take_along_axis(last, within, axis=1))
        for first, last in halves
    ]
    columns = [jnp.where(low, first, last) for first, last in found]
    return [
        jnp.concatenate(columns[j : j + 2], axis=0).astype(jnp.bfloat16)
        for j in range(0, len(columns), 2)
    ]


def table_rows(table, base):
    return [
        tuple(table[half, pl.ds(base + j, 8, stride=8), :] for half in range(2)) for j in range(8)
    ]


def fill_table(table, columns):
    table[0] = columns[:, :LANES]
    table[1] = columns[:, LANES:]


def route_kernel(owner_lanes, owner_ref, lists_ref, queries_ref, out_ref, prefix_ref, place_ref):
    lists = lists_ref[...]
    probes, count = lists.shape
    width = queries_ref.shape[1]
    clusters = owner_ref.shape[0]
    places = clusters * CAPACITY
    ids = lax.broadcasted_iota(jnp.int32, (clusters, count), 0)
    names = [lists[entry : entry + 1, :] == ids for entry in range(probes)]
    named = sum(name.astype(jnp.float32) for name in names)
    before = lax.broadcasted_iota(jnp.int32, (count, count), 0)
    after = lax.broadcasted_iota(jnp.int32, (count, count), 1)
    rank = jnp.dot(named, (before < after).astype(jnp.float32), preferred_element_type=jnp.float32)
    place = lax.broadcasted_iota(jnp.int32, (places, clusters), 0)
    stored = (owner_lanes[...] == place // CAPACITY).astype(jnp.float32)
    named_at = jnp.dot(stored, named, preferred_element_type=jnp.float32)
    rank_at = jnp.dot(stored, rank, preferred_element_type=jnp.float32)
    turn = (lax.broadcasted_iota(jnp.int32, (places, count), 0) % CAPACITY).astype(jnp.float32)
    routing = jnp.where(rank_at == turn, named_at, 0.0).astype(jnp.bfloat16)
    lane = lax.broadcasted_iota(jnp.int32, (count, LANES), 1)
    source = lane // 64 * 64 + lane % 8 * 8 + lane // 8 % 8
    for first in range(0, width, LANES):
        piece = queries_ref[:, first : first + LANES].astype(jnp.float32)
        piece = jnp.take_along_axis(piece, source, axis=1).astype(jnp.bfloat16)
        out_ref[:, first : first + LANES] = jnp.dot(
            routing, piece, preferred_element_type=jnp.float32
        ).astype(jnp.bfloat16)
        if first == 0:
            prefix_ref[...] = piece[:, :PREFIX]
    slots = jnp.zeros(lists.shape, jnp.int32)
    for cluster in range(clusters):
        slots = jnp.where(lists == cluster, owner_ref[cluster], slots)
    ranks = jnp.concatenate(
        [jnp.sum(jnp.where(name, rank, 0.0), axis=0, keepdims=True) for name in names], axis=0
    )
    target = (slots * CAPACITY).astype(jnp.float32) + ranks
    items = count * probes
    row = lax.broadcasted_iota(jnp.int32, (items, probes), 0)
    entry = lax.broadcasted_iota(jnp.int32, (items, probes), 1)
    pick = (row % probes == entry).astype(jnp.float32)
    spread = jnp.dot(pick, target, preferred_element_type=jnp.float32)
    row = lax.broadcasted_iota(jnp.int32, (items, count), 0)
    query = lax.broadcasted_iota(jnp.int32, (items, count), 1)
    target = jnp.sum(jnp.where(row // probes == query, spread, 0.0), axis=1, keepdims=True)
    place = lax.broadcasted_iota(jnp.int32, place_ref.shape, 1)
    place_ref[...] = (place == target.astype(jnp.int32)).astype(jnp.float32)


def rebuild_kernel(counts_ref, codes_ref, codebook_ref, first_ref, second_ref, table):
    fill_table(table, codebook_ref[...].astype(jnp.float32).T)

    def step(index, carry):
        first = pl.multiple_of(index * 8, 8)
        base = pl.multiple_of(index * 64, 64)
        halves = table_rows(table, base)
        for local_id, out_ref in enumerate((first_ref, second_ref)):
            for start in range(0, codes_ref.shape[2], LANES):
                codes = codes_ref[local_id, pl.ds(first, 8), start : start + LANES]
                filled = start < BLOCK * counts_ref[local_id]
                for number, tile in enumerate(looked_up(halves, codes)):
                    out_ref[pl.ds(base + number * 16, 16), start : start + LANES] = jnp.where(
                        filled, tile, jnp.zeros_like(tile)
                    )
        return carry

    lax.fori_loop(0, codes_ref.shape[1] // 8, step, 0, unroll=True)


def coarse_kernel(prefix_ref, codes_ref, codebook_ref, out_ref, table, rebuilt):
    @pl.when(pl.program_id(0) == 0)
    def _():
        fill_table(table, codebook_ref[...].astype(jnp.float32))

    halves = table_rows(table, 0)
    for start in range(0, codes_ref.shape[1], LANES):
        tiles = looked_up(halves, codes_ref[:, start : start + LANES])
        for number, tile in enumerate(tiles):
            rebuilt[number * 16 : number * 16 + 16, start : start + LANES] = tile
    out_ref[...] = jnp.dot(prefix_ref[...], rebuilt[...], preferred_element_type=jnp.float32)


def body(
    queries,
    fine_codebook,
    coarse_codebook,
    fine_codes,
    coarse_codes,
    shortlist,
    owner,
    block_counts,
):
    shards = lax.axis_size("shard")
    groups = lax.axis_size("group")
    local_count, subspaces, row_count = fine_codes.shape
    per_device, width = queries.shape[1:]
    probes = shortlist.shape[2]
    clusters = owner.shape[0]
    centers = fine_codebook.shape[0]
    slab_subspaces, slab_rows = coarse_codes.shape
    positions = clusters * CAPACITY
    queries = queries[0]
    lists = shortlist[0]

    whole = pl.BlockSpec(memory_space=pltpu.VMEM)
    outgoing, prefix, place = pl.pallas_call(
        route_kernel,
        in_specs=[whole, pl.BlockSpec(memory_space=pltpu.SMEM), whole, whole],
        out_shape=[
            jax.ShapeDtypeStruct((positions, width), jnp.bfloat16),
            jax.ShapeDtypeStruct((per_device, PREFIX), jnp.bfloat16),
            jax.ShapeDtypeStruct((per_device * probes, positions), jnp.float32),
        ],
        name="route",
    )(owner.reshape(1, clusters), owner, lists.T, queries)
    arrived = lax.all_to_all(
        outgoing.reshape(shards, positions // shards, width), "shard", 0, 0, tiled=True
    ).reshape(positions, width)

    span = CHUNK * (width // subspaces)
    rebuilt_block = pl.BlockSpec((span, row_count), lambda i: (i, 0))
    rebuilt_shape = jax.ShapeDtypeStruct((width, row_count), jnp.bfloat16)
    rebuilt = pl.pallas_call(
        rebuild_kernel,
        grid=(subspaces // CHUNK,),
        in_specs=[
            pl.BlockSpec(memory_space=pltpu.SMEM),
            pl.BlockSpec((local_count, CHUNK, row_count), lambda i: (0, i, 0)),
            pl.BlockSpec((centers, span), lambda i: (0, i)),
        ],
        out_specs=[rebuilt_block, rebuilt_block],
        out_shape=[rebuilt_shape, rebuilt_shape],
        scratch_shapes=[pltpu.VMEM((2, span, LANES), jnp.float32)],
        cost_estimate=pl.CostEstimate(
            flops=1_000_000, bytes_accessed=100_000, transcendentals=0
        ),
        name="rebuild",
    )(block_counts, fine_codes, fine_codebook)

    def from_group(value, offset):
        pairs = [((i + offset) % groups, i) for i in range(groups)]
        return lax.ppermute(value, "group", pairs)

    near = jnp.concatenate([from_group(prefix, -1), prefix, from_group(prefix, 1)], axis=0)
    around = jnp.concatenate(
        [from_group(near, -3), near, from_group(near[: 2 * per_device], 3)], axis=0
    ).reshape(groups, per_device, PREFIX)
    first = lax.axis_index("group") + groups // 2
    prefixes = jnp.roll(around, first, axis=0).reshape(groups * per_device, PREFIX)
    coarse_scores = pl.pallas_call(
        coarse_kernel,
        grid=(slab_rows // SPAN,),
        in_specs=[
            pl.BlockSpec((groups * per_device, PREFIX), lambda i: (0, 0)),
            pl.BlockSpec((slab_subspaces, SPAN), lambda i: (0, i)),
            pl.BlockSpec((PREFIX, centers), lambda i: (0, 0)),
        ],
        out_specs=pl.BlockSpec((groups * per_device, SPAN), lambda i: (0, i)),
        out_shape=jax.ShapeDtypeStruct((groups * per_device, slab_rows), jnp.float32),
        scratch_shapes=[
            pltpu.VMEM((2, PREFIX, LANES), jnp.float32),
            pltpu.VMEM((PREFIX, SPAN), jnp.bfloat16),
        ],
        cost_estimate=pl.CostEstimate(
            flops=1_000_000, bytes_accessed=100_000, transcendentals=0
        ),
        name="coarse",
    )(prefixes, coarse_codes, coarse_codebook.T)

    scores = [
        jnp.dot(arrived, columns, preferred_element_type=jnp.float32) for columns in rebuilt
    ]
    local = (jnp.arange(positions) // CAPACITY % local_count)[:, None]
    computed = jnp.where(local == 0, scores[0], scores[1])
    returned = lax.all_to_all(
        computed.reshape(shards, positions // shards, row_count), "shard", 0, 0, tiled=True
    ).reshape(positions, row_count)
    fine_scores = jnp.dot(
        place, returned, precision=lax.Precision.HIGHEST, preferred_element_type=jnp.float32
    )
    return (
        coarse_scores.reshape(groups, per_device, slab_rows),
        fine_scores.reshape(1, per_device, probes, row_count),
    )


def solution(mesh):
    in_specs = (
        P("group", "shard", None),
        P(),
        P(),
        P("shard", None, None),
        P(None, "group"),
        P("group", "shard", None),
        P(),
        P("shard"),
    )
    out_specs = (P(None, "shard", "group"), P("group", "shard", None, None))
    return jax.shard_map(body, mesh=mesh, in_specs=in_specs, out_specs=out_specs, check_vma=False)
```

time: 57.2 us -> 50.3 us (0.88)
  Pallas kernels: 17.3 us -> 10.3 us
  matrix products: 0 us -> 3.74 us
  local copies, waits for them, and re-layouts: 2.66 us -> 0.05 us
  waiting for transfers between devices: 4.92 us -> 7.27 us
  other arithmetic: 2.39 us -> 0.7 us
  starting transfers between devices: 28.3 us -> 27 us
    dot_general x0 -> x3, matrix products: none -> 3.74 us  [the longest x2 2.8 us: body(): jnp.dot(arrived, columns, preferred_element_type=jnp.float32)]
    pallas_call x2 -> x1, Pallas kernels: 5.85 us -> 2.57 us  [body(): pl.pallas_call(route_kernel, in_specs=[whole, pl.BlockSpec(memory_space=p...]
    pallas_call x1, Pallas kernels: 5.71 us -> 2.91 us  [body(): pl.pallas_call(coarse_kernel, grid=(slab_rows // SPAN,), in_specs=[pl.Blo...]
    all_to_all x1, waiting for transfers between devices: 2.57 us -> 5.27 us  [body(): lax.all_to_all(computed.reshape(shards, positions // shards, row_count),...]
    select_n x5 -> x0, other arithmetic: 1.46 us -> none  [the longest x2 0.75 us: body(): fine_scores = jnp.take(returned, target, axis=0)]
    all_to_all x1, starting transfers between devices: 9.11 us -> 8.03 us  [body(): lax.all_to_all(computed.reshape(shards, positions // shards, row_count),...]
    unnamed x7 -> x10, local copies, waits for them, and re-layouts: 1.04 us -> 0.04 us
    ppermute x3 -> x4, waiting for transfers between devices: 2.35 us -> 1.39 us  [from_group(): return lax.ppermute(value, 'group', pairs)]
  transfers between devices with their start and end apart: 5 -> 6, of which waited for: 3 -> 3; matrix products, arithmetic and copies ran while one was open for 3% -> 7% of each run, Pallas kernels for 25% -> 16%
where the time goes in v2:
time: 50.3 us; the launch traced here: 49.8 us
  starting transfers between devices  27 us (54%)
  Pallas kernels  10.3 us (20%)
  waiting for transfers between devices  7.27 us (14%)
  matrix products  3.74 us (7%)
  between operations  0.71 us (1%)
  other arithmetic  0.7 us (1%)
    ppermute x4, starting transfers between devices, from_group(): return lax.ppermute(value, 'group', pairs)  10.3 us
    all_to_all x1, starting transfers between devices, body(): lax.all_to_all(outgoing.reshape(shards, positions // shards, width), 'sha...  8.72 us
    all_to_all x1, starting transfers between devices, body(): lax.all_to_all(computed.reshape(shards, positions // shards, row_count),...  8.03 us
    all_to_all x1, waiting for transfers between devices, body(): lax.all_to_all(computed.reshape(shards, positions // shards, row_count),...  5.27 us
    pallas_call x1, Pallas kernels, body(): pl.pallas_call(rebuild_kernel, grid=(subspaces // CHUNK,), in_specs=[pl.B...  4.82 us
    pallas_call x1, Pallas kernels, body(): pl.pallas_call(coarse_kernel, grid=(slab_rows // SPAN,), in_specs=[pl.Blo...  2.91 us
    dot_general x2, matrix products, body(): jnp.dot(arrived, columns, preferred_element_type=jnp.float32)  2.8 us
    pallas_call x1, Pallas kernels, body(): pl.pallas_call(route_kernel, in_specs=[whole, pl.BlockSpec(memory_space=p...  2.57 us
  transfers between devices with their start and end apart: 6, of which 3 were waited for; matrix products, arithmetic and copies ran while one was open for 7% of the time, Pallas kernels for 16%

profile of v2, /device:TPU:1, one launch (start us, length us, event | category | flops | bytes accessed | tf_op | source)
XLA Modules:
  0.0 49.8 jit_solution(4601481501476206935)
XLA Ops:
  0.6 2.6 %route.1 = (bf16[256,2048]{1,0:T(8,128)(2,1)}, bf16[16,64]{1,0:T(8,128)(2,1)}, f32[128,256]{1,0:T(8,128)}) custom-call(s32[1,64]{1,0:T(1,128)} %bitcast.36, s32[64]{0:T(128)} %owner_ref.1, s32[8,16]{1,0:T(8,128)} %bitcast.35, bf16[16,2048]{1,0:T(8,128)(2,1)} %bitcast.32), custom_call_target="tpu_custom_call" | custom-call | tf_op jit(solution)/shard_map/route/pallas_call | solution.py:146
  3.2 0.0 copy-start.2
  3.2 8.7 %all-to-all-start = ((bf16[32,8,2048]{2,1,0:T(8,128)(2,1)}), bf16[32,8,2048]{2,1,0:T(8,128)(2,1)S(1)}, u32[]{:S(2)}, u32[]{:S(2)}) async-start(bf16[32,8,2048]{2,1,0:T(8,128)(2,1)} %bitcast.30), calls=%async_computation | async-start | bytes 2097152 | tf_op jit(solution)/shard_map/all_to_all | solution.py:156
  11.9 0.0 copy-done.2
  11.9 1.7 %collective-permute-start = (bf16[16,64]{1,0:T(8,128)(2,1)S(1)}, bf16[16,64]{1,0:T(8,128)(2,1)S(1)}, u32[]{:S(2)}, u32[]{:S(2)}) collective-permute-start(bf16[16,64]{1,0:T(8,128)(2,1)S(1)} %copy-done.2), channel_id=1, source_target_pairs={{224,0},{0,32},{32,64},{64,96},{96,128},{128,160},{160,192},{192,2... | collective-permute-start | bytes 6152 | tf_op jit(solution)/shard_map/ppermute | solution.py:182
  13.6 4.0 %collective-permute-start.1 = (bf16[16,64]{1,0:T(8,128)(2,1)S(1)}, bf16[16,64]{1,0:T(8,128)(2,1)S(1)}, u32[]{:S(2)}, u32[]{:S(2)}) collective-permute-start(bf16[16,64]{1,0:T(8,128)(2,1)S(1)} %copy-done.2), channel_id=1, source_target_pairs={{32,0},{64,32},{96,64},{128,96},{160,128},{192,160},{224,192},{0,2... | collective-permute-start | bytes 6152 | tf_op jit(solution)/shard_map/ppermute | solution.py:182
  17.7 4.8 %rebuild.1 = (bf16[2048,256]{1,0:T(8,128)(2,1)}, bf16[2048,256]{1,0:T(8,128)(2,1)}) custom-call(s32[2]{0:T(128)} %counts_ref.1, s32[2,256,256]{2,1,0:T(8,128)} %codes_ref.3, bf16[256,2048]{1,0:T(8,128)(2,1)} %codebook_ref.1), custom_call_target="tpu_custom_call" | custom-call | flops 1000000 | bytes 100000 | tf_op jit(solution)/shard_map/rebuild/pallas_call | solution.py:163
  22.5 0.0 copy-start
  22.5 0.0 collective-permute-done
  22.5 0.0 collective-permute-done.1
  22.5 1.6 %collective-permute-start.2 = (bf16[48,64]{1,0:T(8,128)(2,1)S(1)}, bf16[48,64]{1,0:T(8,128)(2,1)S(1)}, u32[]{:S(2)}, u32[]{:S(2)}) collective-permute-start(bf16[48,64]{1,0:T(8,128)(2,1)S(1)} %pad_maximum_fusion), channel_id=1, source_target_pairs={{160,0},{192,32},{224,64},{0,96},{32,128},{64,160},{96,192},{128,2... | collective-permute-start | bytes 18440 | tf_op jit(solution)/shard_map/ppermute | solution.py:182
  24.2 2.9 %collective-permute-start.3 = (bf16[32,64]{1,0:T(8,128)(2,1)S(1)}, bf16[32,64]{1,0:T(8,128)(2,1)S(1)}, u32[]{:S(2)}, u32[]{:S(2)}) collective-permute-start(bf16[32,64]{1,0:T(8,128)(2,1)S(1)} %pad_maximum_fusion.1), channel_id=1, source_target_pairs={{96,0},{128,32},{160,64},{192,96},{224,128},{0,160},{32,192},{64,2... | collective-permute-start | bytes 12296 | tf_op jit(solution)/shard_map/ppermute | solution.py:182
  27.1 1.4 %collective-permute-done.2 = bf16[48,64]{1,0:T(8,128)(2,1)S(1)} collective-permute-done((bf16[48,64]{1,0:T(8,128)(2,1)S(1)}, bf16[48,64]{1,0:T(8,128)(2,1)S(1)}, u32[]{:S(2)}, u32[]{:S(2)}) %collective-permute-start.2) | collective-permute-done | bytes 6176 | tf_op jit(solution)/shard_map/ppermute | solution.py:182
  28.5 0.6 %all-to-all-done = bf16[32,8,2048]{2,1,0:T(8,128)(2,1)S(1)} async-done(((bf16[32,8,2048]{2,1,0:T(8,128)(2,1)}), bf16[32,8,2048]{2,1,0:T(8,128)(2,1)S(1)}, u32[]{:S(2)}, u32[]{:S(2)}) %all-to-all-start) | async-done | bytes 1048608 | tf_op jit(solution)/shard_map/all_to_all | solution.py:156
  29.1 1.7 %fusion.2 = f32[256,256]{1,0:T(8,128)S(1)} fusion(bf16[2048,256]{1,0:T(8,128)(2,1)} %get-tuple-element.10, bf16[32,8,2048]{2,1,0:T(8,128)(2,1)S(1)} %all-to-all-done), kind=kOutput, calls=%fused_computation.4 | convolution fusion | flops 268435456 | bytes 2359296 | tf_op jit(solution)/shard_map/dot_general | solution.py:211
  30.8 0.0 copy-done
  30.8 1.1 %fusion = f32[32,8,256]{2,1,0:T(8,128)} fusion(f32[256,256]{1,0:T(8,128)S(1)} %fusion.2, bf16[2048,256]{1,0:T(8,128)(2,1)S(1)} %copy-done, bf16[32,8,2048]{2,1,0:T(8,128)(2,1)S(1)} %all-to-all-done, pred[256]{0:T(512)(128)(4,1)S(1)} %fusion.8), kind=kOutput, calls=%fused_computation.1 | convolution fusion | flops 268500992 | bytes 2621696 | tf_op jit(solution)/shard_map/dot_general | solution.py:211
  31.9 8.0 %all-to-all-start.1 = ((f32[32,8,256]{2,1,0:T(8,128)}), f32[32,8,256]{2,1,0:T(8,128)S(1)}, u32[]{:S(2)}, u32[]{:S(2)}) async-start(f32[32,8,256]{2,1,0:T(8,128)} %fusion), calls=%async_computation.1 | async-start | bytes 524288 | tf_op jit(solution)/shard_map/all_to_all | solution.py:215
  40.0 0.0 collective-permute-done.3
  40.0 0.7 %fusion.6 = bf16[8,16,64]{2,1,0:T(8,128)(2,1)} fusion(s32[]{:T(128)S(6)} %select_n.37, bf16[8,16,64]{2,1,0:T(8,128)(2,1)S(1)} %bitcast.33), kind=kLoop, calls=%fused_computation.10 | loop fusion | flops 8192 | bytes 32772 | tf_op jit(solution)/shard_map/jit(_roll_dynamic)/concatenate | solution.py:189
  40.7 2.9 %coarse.1 = f32[128,4096]{1,0:T(8,128)} custom-call(bf16[128,64]{1,0:T(8,128)(2,1)} %bitcast.31, s32[8,4096]{1,0:T(8,128)} %codes_ref.2, bf16[64,256]{1,0:T(8,128)(2,1)} %bitcast.34), custom_call_target="tpu_custom_call" | custom-call | flops 1000000 | bytes 100000 | tf_op jit(solution)/shard_map/coarse/pallas_call | solution.py:190
  43.6 5.3 %all-to-all-done.1 = f32[32,8,256]{2,1,0:T(8,128)S(1)} async-done(((f32[32,8,256]{2,1,0:T(8,128)}), f32[32,8,256]{2,1,0:T(8,128)S(1)}, u32[]{:S(2)}, u32[]{:S(2)}) %all-to-all-start.1) | async-done | bytes 262176 | tf_op jit(solution)/shard_map/all_to_all | solution.py:215
  48.9 0.0 copy-done.1
  48.9 0.9 %convolution_bitcast_fusion = f32[1,16,8,256]{3,2,1,0:T(8,128)} fusion(f32[32,8,256]{2,1,0:T(8,128)S(1)} %all-to-all-done.1, f32[128,256]{1,0:T(8,128)S(1)} %copy-done.1), kind=kOutput, calls=%fused_computation.2 | convolution fusion | flops 100663296 | bytes 524288 | tf_op jit(solution)/shard_map/dot_general | solution.py:218
  (9 shorter events, 0.1 us)
Async XLA Ops:
  3.2 8.7 %copy-start.2 = (bf16[16,64]{1,0:T(8,128)(2,1)S(1)}, bf16[16,64]{1,0:T(8,128)(2,1)}, u32[]{:S(2)}) copy-start(bf16[16,64]{1,0:T(8,128)(2,1)} %get-tuple-element.7) | copy-start | bytes 6148
  3.2 25.9 %all-to-all-start = ((bf16[32,8,2048]{2,1,0:T(8,128)(2,1)}), bf16[32,8,2048]{2,1,0:T(8,128)(2,1)S(1)}, u32[]{:S(2)}, u32[]{:S(2)}) async-start(bf16[32,8,2048]{2,1,0:T(8,128)(2,1)} %bitcast.30), calls=%async_computation | async-start | bytes 2097152 | tf_op jit(solution)/shard_map/all_to_all | solution.py:156
  11.9 10.6 %collective-permute-start = (bf16[16,64]{1,0:T(8,128)(2,1)S(1)}, bf16[16,64]{1,0:T(8,128)(2,1)S(1)}, u32[]{:S(2)}, u32[]{:S(2)}) collective-permute-start(bf16[16,64]{1,0:T(8,128)(2,1)S(1)} %copy-done.2), channel_id=1, source_target_pairs={{224,0},{0,32},{32,64},{64,96},{96,128},{128,160},{160,192},{192,2... | collective-permute-start | bytes 6152 | tf_op jit(solution)/shard_map/ppermute | solution.py:182
  13.6 8.9 %collective-permute-start.1 = (bf16[16,64]{1,0:T(8,128)(2,1)S(1)}, bf16[16,64]{1,0:T(8,128)(2,1)S(1)}, u32[]{:S(2)}, u32[]{:S(2)}) collective-permute-start(bf16[16,64]{1,0:T(8,128)(2,1)S(1)} %copy-done.2), channel_id=1, source_target_pairs={{32,0},{64,32},{96,64},{128,96},{160,128},{192,160},{224,192},{0,2... | collective-permute-start | bytes 6152 | tf_op jit(solution)/shard_map/ppermute | solution.py:182
  22.5 8.3 %copy-start = (bf16[2048,256]{1,0:T(8,128)(2,1)S(1)}, bf16[2048,256]{1,0:T(8,128)(2,1)}, u32[]{:S(2)}) copy-start(bf16[2048,256]{1,0:T(8,128)(2,1)} %get-tuple-element.11) | copy-start | bytes 3145732
  22.5 5.9 %collective-permute-start.2 = (bf16[48,64]{1,0:T(8,128)(2,1)S(1)}, bf16[48,64]{1,0:T(8,128)(2,1)S(1)}, u32[]{:S(2)}, u32[]{:S(2)}) collective-permute-start(bf16[48,64]{1,0:T(8,128)(2,1)S(1)} %pad_maximum_fusion), channel_id=1, source_target_pairs={{160,0},{192,32},{224,64},{0,96},{32,128},{64,160},{96,192},{128,2... | collective-permute-start | bytes 18440 | tf_op jit(solution)/shard_map/ppermute | solution.py:182
  24.2 15.8 %collective-permute-start.3 = (bf16[32,64]{1,0:T(8,128)(2,1)S(1)}, bf16[32,64]{1,0:T(8,128)(2,1)S(1)}, u32[]{:S(2)}, u32[]{:S(2)}) collective-permute-start(bf16[32,64]{1,0:T(8,128)(2,1)S(1)} %pad_maximum_fusion.1), channel_id=1, source_target_pairs={{96,0},{128,32},{160,64},{192,96},{224,128},{0,160},{32,192},{64,2... | collective-permute-start | bytes 12296 | tf_op jit(solution)/shard_map/ppermute | solution.py:182
  31.9 16.9 %copy-start.1 = (f32[128,256]{1,0:T(8,128)S(1)}, f32[128,256]{1,0:T(8,128)}, u32[]{:S(2)}) copy-start(f32[128,256]{1,0:T(8,128)} %get-tuple-element.8) | copy-start | bytes 393220
  31.9 16.9 %all-to-all-start.1 = ((f32[32,8,256]{2,1,0:T(8,128)}), f32[32,8,256]{2,1,0:T(8,128)S(1)}, u32[]{:S(2)}, u32[]{:S(2)}) async-start(f32[32,8,256]{2,1,0:T(8,128)} %fusion), calls=%async_computation.1 | async-start | bytes 524288 | tf_op jit(solution)/shard_map/all_to_all | solution.py:215

commit v3 on v2

--- a/solution.py
+++ b/solution.py
@@ -212,11 +212,12 @@
     ]
     local = (jnp.arange(positions) // CAPACITY % local_count)[:, None]
     computed = jnp.where(local == 0, scores[0], scores[1])
+    computed = computed.astype(jnp.bfloat16)
     returned = lax.all_to_all(
         computed.reshape(shards, positions // shards, row_count), "shard", 0, 0, tiled=True
     ).reshape(positions, row_count)
     fine_scores = jnp.dot(
-        place, returned, precision=lax.Precision.HIGHEST, preferred_element_type=jnp.float32
+        place.astype(jnp.bfloat16), returned, preferred_element_type=jnp.float32
     )
     return (
         coarse_scores.reshape(groups, per_device, slab_rows),

time: 50.3 us -> 48.8 us (0.970)
  waiting for transfers between devices: 7.27 us -> 6 us
    all_to_all x1, waiting for transfers between devices: 5.27 us -> 4.01 us  [body(): lax.all_to_all(computed.reshape(shards, positions // shards, row_count),...]
where the time goes in v3:
time: 48.8 us; the launch traced here: 48.3 us
  starting transfers between devices  26.9 us (55%)
  Pallas kernels  10.3 us (21%)
  waiting for transfers between devices  6 us (12%)
  matrix products  3.58 us (7%)
  between operations  0.72 us (1%)
  other arithmetic  0.7 us (1%)
    ppermute x4, starting transfers between devices, from_group(): return lax.ppermute(value, 'group', pairs)  10.3 us
    all_to_all x1, starting transfers between devices, body(): lax.all_to_all(outgoing.reshape(shards, positions // shards, width), 'sha...  8.72 us
    all_to_all x1, starting transfers between devices, body(): lax.all_to_all(computed.reshape(shards, positions // shards, row_count),...  7.92 us
    pallas_call x1, Pallas kernels, body(): pl.pallas_call(rebuild_kernel, grid=(subspaces // CHUNK,), in_specs=[pl.B...  4.82 us
    all_to_all x1, waiting for transfers between devices, body(): lax.all_to_all(computed.reshape(shards, positions // shards, row_count),...  4.01 us
    pallas_call x1, Pallas kernels, body(): pl.pallas_call(coarse_kernel, grid=(slab_rows // SPAN,), in_specs=[pl.Blo...  2.91 us
    dot_general x2, matrix products, body(): jnp.dot(arrived, columns, preferred_element_type=jnp.float32)  2.75 us
    pallas_call x1, Pallas kernels, body(): pl.pallas_call(route_kernel, in_specs=[whole, pl.BlockSpec(memory_space=p...  2.57 us
  transfers between devices with their start and end apart: 6, of which 3 were waited for; matrix products, arithmetic and copies ran while one was open for 7% of the time, Pallas kernels for 16%

profile of v3, /device:TPU:1, one launch (start us, length us, event | category | flops | bytes accessed | tf_op | source)
XLA Modules:
  0.0 48.3 jit_solution(4522995778151430281)
XLA Ops:
  0.6 2.6 %route.1 = (bf16[256,2048]{1,0:T(8,128)(2,1)}, bf16[16,64]{1,0:T(8,128)(2,1)}, f32[128,256]{1,0:T(8,128)}) custom-call(s32[1,64]{1,0:T(1,128)} %bitcast.36, s32[64]{0:T(128)} %owner_ref.1, s32[8,16]{1,0:T(8,128)} %bitcast.35, bf16[16,2048]{1,0:T(8,128)(2,1)} %bitcast.32), custom_call_target="tpu_custom_call" | custom-call | tf_op jit(solution)/shard_map/route/pallas_call | solution.py:146
  3.2 0.0 copy-start.1
  3.2 8.7 %all-to-all-start = ((bf16[32,8,2048]{2,1,0:T(8,128)(2,1)}), bf16[32,8,2048]{2,1,0:T(8,128)(2,1)S(1)}, u32[]{:S(2)}, u32[]{:S(2)}) async-start(bf16[32,8,2048]{2,1,0:T(8,128)(2,1)} %bitcast.30), calls=%async_computation | async-start | bytes 2097152 | tf_op jit(solution)/shard_map/all_to_all | solution.py:156
  11.9 0.0 copy-done.1
  11.9 1.7 %collective-permute-start = (bf16[16,64]{1,0:T(8,128)(2,1)S(1)}, bf16[16,64]{1,0:T(8,128)(2,1)S(1)}, u32[]{:S(2)}, u32[]{:S(2)}) collective-permute-start(bf16[16,64]{1,0:T(8,128)(2,1)S(1)} %copy-done.1), channel_id=1, source_target_pairs={{224,0},{0,32},{32,64},{64,96},{96,128},{128,160},{160,192},{192,2... | collective-permute-start | bytes 6152 | tf_op jit(solution)/shard_map/ppermute | solution.py:182
  13.6 4.0 %collective-permute-start.1 = (bf16[16,64]{1,0:T(8,128)(2,1)S(1)}, bf16[16,64]{1,0:T(8,128)(2,1)S(1)}, u32[]{:S(2)}, u32[]{:S(2)}) collective-permute-start(bf16[16,64]{1,0:T(8,128)(2,1)S(1)} %copy-done.1), channel_id=1, source_target_pairs={{32,0},{64,32},{96,64},{128,96},{160,128},{192,160},{224,192},{0,2... | collective-permute-start | bytes 6152 | tf_op jit(solution)/shard_map/ppermute | solution.py:182
  17.7 4.8 %rebuild.1 = (bf16[2048,256]{1,0:T(8,128)(2,1)}, bf16[2048,256]{1,0:T(8,128)(2,1)}) custom-call(s32[2]{0:T(128)} %counts_ref.1, s32[2,256,256]{2,1,0:T(8,128)} %codes_ref.3, bf16[256,2048]{1,0:T(8,128)(2,1)} %codebook_ref.1), custom_call_target="tpu_custom_call" | custom-call | flops 1000000 | bytes 100000 | tf_op jit(solution)/shard_map/rebuild/pallas_call | solution.py:163
  22.5 0.0 collective-permute-done
  22.5 0.0 collective-permute-done.1
  22.5 1.6 %collective-permute-start.2 = (bf16[48,64]{1,0:T(8,128)(2,1)S(1)}, bf16[48,64]{1,0:T(8,128)(2,1)S(1)}, u32[]{:S(2)}, u32[]{:S(2)}) collective-permute-start(bf16[48,64]{1,0:T(8,128)(2,1)S(1)} %pad_maximum_fusion), channel_id=1, source_target_pairs={{160,0},{192,32},{224,64},{0,96},{32,128},{64,160},{96,192},{128,2... | collective-permute-start | bytes 18440 | tf_op jit(solution)/shard_map/ppermute | solution.py:182
  24.2 2.9 %collective-permute-start.3 = (bf16[32,64]{1,0:T(8,128)(2,1)S(1)}, bf16[32,64]{1,0:T(8,128)(2,1)S(1)}, u32[]{:S(2)}, u32[]{:S(2)}) collective-permute-start(bf16[32,64]{1,0:T(8,128)(2,1)S(1)} %pad_maximum_fusion.1), channel_id=1, source_target_pairs={{96,0},{128,32},{160,64},{192,96},{224,128},{0,160},{32,192},{64,2... | collective-permute-start | bytes 12296 | tf_op jit(solution)/shard_map/ppermute | solution.py:182
  27.1 1.4 %collective-permute-done.2 = bf16[48,64]{1,0:T(8,128)(2,1)S(1)} collective-permute-done((bf16[48,64]{1,0:T(8,128)(2,1)S(1)}, bf16[48,64]{1,0:T(8,128)(2,1)S(1)}, u32[]{:S(2)}, u32[]{:S(2)}) %collective-permute-start.2) | collective-permute-done | bytes 6176 | tf_op jit(solution)/shard_map/ppermute | solution.py:182
  28.5 0.6 %all-to-all-done = bf16[32,8,2048]{2,1,0:T(8,128)(2,1)S(1)} async-done(((bf16[32,8,2048]{2,1,0:T(8,128)(2,1)}), bf16[32,8,2048]{2,1,0:T(8,128)(2,1)S(1)}, u32[]{:S(2)}, u32[]{:S(2)}) %all-to-all-start) | async-done | bytes 1048608 | tf_op jit(solution)/shard_map/all_to_all | solution.py:156
  29.1 1.7 %fusion.3 = bf16[256,256]{1,0:T(8,128)(2,1)S(1)} fusion(bf16[2048,256]{1,0:T(8,128)(2,1)} %get-tuple-element.10, bf16[32,8,2048]{2,1,0:T(8,128)(2,1)S(1)} %all-to-all-done), kind=kOutput, calls=%fused_computation.5 | convolution fusion | flops 268435456 | bytes 2228224 | tf_op jit(solution)/shard_map/dot_general | solution.py:211
  30.8 0.0 copy-done.2
  30.8 0.0 copy-start
  30.8 1.1 %fusion.1 = bf16[32,8,256]{2,1,0:T(8,128)(2,1)} fusion(bf16[256,256]{1,0:T(8,128)(2,1)S(1)} %fusion.3, bf16[2048,256]{1,0:T(8,128)(2,1)S(1)} %copy-done.2, bf16[32,8,2048]{2,1,0:T(8,128)(2,1)S(1)} %all-to-all-done, pred[256]{0:T(512)(128)(4,1)S(1)} %fusion.10), kind=kOutput, calls=%fused_computation.2 | convolution fusion | flops 268500992 | bytes 2359552 | tf_op jit(solution)/shard_map/dot_general | solution.py:211
  31.9 7.9 %all-to-all-start.1 = ((bf16[32,8,256]{2,1,0:T(8,128)(2,1)}), bf16[32,8,256]{2,1,0:T(8,128)(2,1)S(1)}, u32[]{:S(2)}, u32[]{:S(2)}) async-start(bf16[32,8,256]{2,1,0:T(8,128)(2,1)} %fusion.1), calls=%async_computation.1 | async-start | bytes 262144 | tf_op jit(solution)/shard_map/all_to_all | solution.py:216
  39.8 0.0 collective-permute-done.3
  39.8 0.7 %fusion.8 = bf16[8,16,64]{2,1,0:T(8,128)(2,1)} fusion(s32[]{:T(128)S(6)} %select_n.37, bf16[8,16,64]{2,1,0:T(8,128)(2,1)S(1)} %bitcast.33), kind=kLoop, calls=%fused_computation.12 | loop fusion | flops 8192 | bytes 32772 | tf_op jit(solution)/shard_map/jit(_roll_dynamic)/concatenate | solution.py:189
  40.5 2.9 %coarse.1 = f32[128,4096]{1,0:T(8,128)} custom-call(bf16[128,64]{1,0:T(8,128)(2,1)} %bitcast.31, s32[8,4096]{1,0:T(8,128)} %codes_ref.2, bf16[64,256]{1,0:T(8,128)(2,1)} %bitcast.34), custom_call_target="tpu_custom_call" | custom-call | flops 1000000 | bytes 100000 | tf_op jit(solution)/shard_map/coarse/pallas_call | solution.py:190
  43.4 4.0 %all-to-all-done.1 = bf16[32,8,256]{2,1,0:T(8,128)(2,1)S(1)} async-done(((bf16[32,8,256]{2,1,0:T(8,128)(2,1)}), bf16[32,8,256]{2,1,0:T(8,128)(2,1)S(1)}, u32[]{:S(2)}, u32[]{:S(2)}) %all-to-all-start.1) | async-done | bytes 131104 | tf_op jit(solution)/shard_map/all_to_all | solution.py:216
  47.4 0.0 copy-done
  47.4 0.8 %convolution_bitcast_fusion = f32[1,16,8,256]{3,2,1,0:T(8,128)} fusion(bf16[32,8,256]{2,1,0:T(8,128)(2,1)S(1)} %all-to-all-done.1, f32[128,256]{1,0:T(8,128)S(1)} %copy-done), kind=kOutput, calls=%fused_computation.3 | convolution fusion | flops 16809984 | bytes 393216 | tf_op jit(solution)/shard_map/dot_general | solution.py:219
  (9 shorter events, 0.1 us)
Async XLA Ops:
  3.2 8.7 %copy-start.1 = (bf16[16,64]{1,0:T(8,128)(2,1)S(1)}, bf16[16,64]{1,0:T(8,128)(2,1)}, u32[]{:S(2)}) copy-start(bf16[16,64]{1,0:T(8,128)(2,1)} %get-tuple-element.7) | copy-start | bytes 6148
  3.2 25.9 %all-to-all-start = ((bf16[32,8,2048]{2,1,0:T(8,128)(2,1)}), bf16[32,8,2048]{2,1,0:T(8,128)(2,1)S(1)}, u32[]{:S(2)}, u32[]{:S(2)}) async-start(bf16[32,8,2048]{2,1,0:T(8,128)(2,1)} %bitcast.30), calls=%async_computation | async-start | bytes 2097152 | tf_op jit(solution)/shard_map/all_to_all | solution.py:156
  11.9 10.6 %collective-permute-start = (bf16[16,64]{1,0:T(8,128)(2,1)S(1)}, bf16[16,64]{1,0:T(8,128)(2,1)S(1)}, u32[]{:S(2)}, u32[]{:S(2)}) collective-permute-start(bf16[16,64]{1,0:T(8,128)(2,1)S(1)} %copy-done.1), channel_id=1, source_target_pairs={{224,0},{0,32},{32,64},{64,96},{96,128},{128,160},{160,192},{192,2... | collective-permute-start | bytes 6152 | tf_op jit(solution)/shard_map/ppermute | solution.py:182
  13.6 8.9 %collective-permute-start.1 = (bf16[16,64]{1,0:T(8,128)(2,1)S(1)}, bf16[16,64]{1,0:T(8,128)(2,1)S(1)}, u32[]{:S(2)}, u32[]{:S(2)}) collective-permute-start(bf16[16,64]{1,0:T(8,128)(2,1)S(1)} %copy-done.1), channel_id=1, source_target_pairs={{32,0},{64,32},{96,64},{128,96},{160,128},{192,160},{224,192},{0,2... | collective-permute-start | bytes 6152 | tf_op jit(solution)/shard_map/ppermute | solution.py:182
  22.5 8.3 %copy-start.2 = (bf16[2048,256]{1,0:T(8,128)(2,1)S(1)}, bf16[2048,256]{1,0:T(8,128)(2,1)}, u32[]{:S(2)}) copy-start(bf16[2048,256]{1,0:T(8,128)(2,1)} %get-tuple-element.11) | copy-start | bytes 3145732
  22.5 5.9 %collective-permute-start.2 = (bf16[48,64]{1,0:T(8,128)(2,1)S(1)}, bf16[48,64]{1,0:T(8,128)(2,1)S(1)}, u32[]{:S(2)}, u32[]{:S(2)}) collective-permute-start(bf16[48,64]{1,0:T(8,128)(2,1)S(1)} %pad_maximum_fusion), channel_id=1, source_target_pairs={{160,0},{192,32},{224,64},{0,96},{32,128},{64,160},{96,192},{128,2... | collective-permute-start | bytes 18440 | tf_op jit(solution)/shard_map/ppermute | solution.py:182
  24.2 15.6 %collective-permute-start.3 = (bf16[32,64]{1,0:T(8,128)(2,1)S(1)}, bf16[32,64]{1,0:T(8,128)(2,1)S(1)}, u32[]{:S(2)}, u32[]{:S(2)}) collective-permute-start(bf16[32,64]{1,0:T(8,128)(2,1)S(1)} %pad_maximum_fusion.1), channel_id=1, source_target_pairs={{96,0},{128,32},{160,64},{192,96},{224,128},{0,160},{32,192},{64,2... | collective-permute-start | bytes 12296 | tf_op jit(solution)/shard_map/ppermute | solution.py:182
  30.8 16.7 %copy-start = (f32[128,256]{1,0:T(8,128)S(1)}, f32[128,256]{1,0:T(8,128)}, u32[]{:S(2)}) copy-start(f32[128,256]{1,0:T(8,128)} %get-tuple-element.8) | copy-start | bytes 393220
  31.9 15.6 %all-to-all-start.1 = ((bf16[32,8,256]{2,1,0:T(8,128)(2,1)}), bf16[32,8,256]{2,1,0:T(8,128)(2,1)S(1)}, u32[]{:S(2)}, u32[]{:S(2)}) async-start(bf16[32,8,256]{2,1,0:T(8,128)(2,1)} %fusion.1), calls=%async_computation.1 | async-start | bytes 262144 | tf_op jit(solution)/shard_map/all_to_all | solution.py:216

commit v4 on v3

--- a/solution.py
+++ b/solution.py
@@ -10,7 +10,7 @@
 PREFIX = 64
 BLOCK = 128
 CAPACITY = 4
-CHUNK = 64
+CHUNK = 128
 SPAN = 2048
 LANES = 128
 
@@ -88,7 +88,7 @@
 
 
 def rebuild_kernel(counts_ref, codes_ref, codebook_ref, first_ref, second_ref, table):
-    fill_table(table, codebook_ref[...].astype(jnp.float32).T)
+    fill_table(table, codebook_ref[...].T.astype(jnp.float32))
 
     def step(index, carry):
         first = pl.multiple_of(index * 8, 8)

time: 48.8 us -> 47.9 us (0.982)
  waiting for transfers between devices: 6 us -> 6.76 us
  Pallas kernels: 10.3 us -> 9.55 us
  starting transfers between devices: 26.9 us -> 26.2 us
    all_to_all x1, waiting for transfers between devices: 0.6 us -> 1.66 us  [body(): lax.all_to_all(outgoing.reshape(shards, positions // shards, width), 'sha...]
    pallas_call x1, Pallas kernels: 4.82 us -> 4.06 us  [body(): pl.pallas_call(rebuild_kernel, grid=(subspaces // CHUNK,), in_specs=[pl.B...]
    all_to_all x1, starting transfers between devices: 7.92 us -> 7.15 us  [body(): lax.all_to_all(computed.reshape(shards, positions // shards, row_count),...]
  transfers between devices with their start and end apart: 6 -> 6, of which waited for: 3 -> 3; matrix products, arithmetic and copies ran while one was open for 7% -> 7% of each run, Pallas kernels for 16% -> 15%
where the time goes in v4:
time: 47.9 us; the launch traced here: 47.5 us
  starting transfers between devices  26.2 us (55%)
  Pallas kernels  9.55 us (20%)
  waiting for transfers between devices  6.76 us (14%)
  matrix products  3.58 us (7%)
  between operations  0.72 us (2%)
  other arithmetic  0.7 us (1%)
    ppermute x4, starting transfers between devices, from_group(): return lax.ppermute(value, 'group', pairs)  10.3 us
    all_to_all x1, starting transfers between devices, body(): lax.all_to_all(outgoing.reshape(shards, positions // shards, width), 'sha...  8.72 us
    all_to_all x1, starting transfers between devices, body(): lax.all_to_all(computed.reshape(shards, positions // shards, row_count),...  7.15 us
    pallas_call x1, Pallas kernels, body(): pl.pallas_call(rebuild_kernel, grid=(subspaces // CHUNK,), in_specs=[pl.B...  4.06 us
    all_to_all x1, waiting for transfers between devices, body(): lax.all_to_all(computed.reshape(shards, positions // shards, row_count),...  4.01 us
    pallas_call x1, Pallas kernels, body(): pl.pallas_call(coarse_kernel, grid=(slab_rows // SPAN,), in_specs=[pl.Blo...  2.91 us
    dot_general x2, matrix products, body(): jnp.dot(arrived, columns, preferred_element_type=jnp.float32)  2.75 us
    pallas_call x1, Pallas kernels, body(): pl.pallas_call(route_kernel, in_specs=[whole, pl.BlockSpec(memory_space=p...  2.57 us
  transfers between devices with their start and end apart: 6, of which 3 were waited for; matrix products, arithmetic and copies ran while one was open for 7% of the time, Pallas kernels for 15%

profile of v4, /device:TPU:1, one launch (start us, length us, event | category | flops | bytes accessed | tf_op | source)
XLA Modules:
  0.0 47.5 jit_solution(10269808962419756900)
XLA Ops:
  0.6 2.6 %route.1 = (bf16[256,2048]{1,0:T(8,128)(2,1)}, bf16[16,64]{1,0:T(8,128)(2,1)}, f32[128,256]{1,0:T(8,128)}) custom-call(s32[1,64]{1,0:T(1,128)} %bitcast.36, s32[64]{0:T(128)} %owner_ref.1, s32[8,16]{1,0:T(8,128)} %bitcast.35, bf16[16,2048]{1,0:T(8,128)(2,1)} %bitcast.32), custom_call_target="tpu_custom_call" | custom-call | tf_op jit(solution)/shard_map/route/pallas_call | solution.py:146
  3.2 0.0 copy-start.1
  3.2 8.7 %all-to-all-start = ((bf16[32,8,2048]{2,1,0:T(8,128)(2,1)}), bf16[32,8,2048]{2,1,0:T(8,128)(2,1)S(1)}, u32[]{:S(2)}, u32[]{:S(2)}) async-start(bf16[32,8,2048]{2,1,0:T(8,128)(2,1)} %bitcast.30), calls=%async_computation | async-start | bytes 2097152 | tf_op jit(solution)/shard_map/all_to_all | solution.py:156
  11.9 0.0 copy-done.1
  11.9 1.7 %collective-permute-start = (bf16[16,64]{1,0:T(8,128)(2,1)S(1)}, bf16[16,64]{1,0:T(8,128)(2,1)S(1)}, u32[]{:S(2)}, u32[]{:S(2)}) collective-permute-start(bf16[16,64]{1,0:T(8,128)(2,1)S(1)} %copy-done.1), channel_id=1, source_target_pairs={{224,0},{0,32},{32,64},{64,96},{96,128},{128,160},{160,192},{192,2... | collective-permute-start | bytes 6152 | tf_op jit(solution)/shard_map/ppermute | solution.py:182
  13.6 4.0 %collective-permute-start.1 = (bf16[16,64]{1,0:T(8,128)(2,1)S(1)}, bf16[16,64]{1,0:T(8,128)(2,1)S(1)}, u32[]{:S(2)}, u32[]{:S(2)}) collective-permute-start(bf16[16,64]{1,0:T(8,128)(2,1)S(1)} %copy-done.1), channel_id=1, source_target_pairs={{32,0},{64,32},{96,64},{128,96},{160,128},{192,160},{224,192},{0,2... | collective-permute-start | bytes 6152 | tf_op jit(solution)/shard_map/ppermute | solution.py:182
  17.7 4.1 %rebuild.1 = (bf16[2048,256]{1,0:T(8,128)(2,1)}, bf16[2048,256]{1,0:T(8,128)(2,1)}) custom-call(s32[2]{0:T(128)} %counts_ref.1, s32[2,256,256]{2,1,0:T(8,128)} %codes_ref.3, bf16[256,2048]{1,0:T(8,128)(2,1)} %codebook_ref.1), custom_call_target="tpu_custom_call" | custom-call | flops 1000000 | bytes 100000 | tf_op jit(solution)/shard_map/rebuild/pallas_call | solution.py:163
  21.7 0.0 collective-permute-done
  21.8 0.0 collective-permute-done.1
  21.8 1.6 %collective-permute-start.2 = (bf16[48,64]{1,0:T(8,128)(2,1)S(1)}, bf16[48,64]{1,0:T(8,128)(2,1)S(1)}, u32[]{:S(2)}, u32[]{:S(2)}) collective-permute-start(bf16[48,64]{1,0:T(8,128)(2,1)S(1)} %pad_maximum_fusion), channel_id=1, source_target_pairs={{160,0},{192,32},{224,64},{0,96},{32,128},{64,160},{96,192},{128,2... | collective-permute-start | bytes 18440 | tf_op jit(solution)/shard_map/ppermute | solution.py:182
  23.4 2.9 %collective-permute-start.3 = (bf16[32,64]{1,0:T(8,128)(2,1)S(1)}, bf16[32,64]{1,0:T(8,128)(2,1)S(1)}, u32[]{:S(2)}, u32[]{:S(2)}) collective-permute-start(bf16[32,64]{1,0:T(8,128)(2,1)S(1)} %pad_maximum_fusion.1), channel_id=1, source_target_pairs={{96,0},{128,32},{160,64},{192,96},{224,128},{0,160},{32,192},{64,2... | collective-permute-start | bytes 12296 | tf_op jit(solution)/shard_map/ppermute | solution.py:182
  26.3 1.1 %collective-permute-done.2 = bf16[48,64]{1,0:T(8,128)(2,1)S(1)} collective-permute-done((bf16[48,64]{1,0:T(8,128)(2,1)S(1)}, bf16[48,64]{1,0:T(8,128)(2,1)S(1)}, u32[]{:S(2)}, u32[]{:S(2)}) %collective-permute-start.2) | collective-permute-done | bytes 6176 | tf_op jit(solution)/shard_map/ppermute | solution.py:182
  27.5 1.7 %all-to-all-done = bf16[32,8,2048]{2,1,0:T(8,128)(2,1)S(1)} async-done(((bf16[32,8,2048]{2,1,0:T(8,128)(2,1)}), bf16[32,8,2048]{2,1,0:T(8,128)(2,1)S(1)}, u32[]{:S(2)}, u32[]{:S(2)}) %all-to-all-start) | async-done | bytes 1048608 | tf_op jit(solution)/shard_map/all_to_all | solution.py:156
  29.1 1.7 %fusion.3 = bf16[256,256]{1,0:T(8,128)(2,1)S(1)} fusion(bf16[2048,256]{1,0:T(8,128)(2,1)} %get-tuple-element.10, bf16[32,8,2048]{2,1,0:T(8,128)(2,1)S(1)} %all-to-all-done), kind=kOutput, calls=%fused_computation.5 | convolution fusion | flops 268435456 | bytes 2228224 | tf_op jit(solution)/shard_map/dot_general | solution.py:211
  30.8 0.0 copy-done.2
  30.8 0.0 copy-start
  30.8 1.1 %fusion.1 = bf16[32,8,256]{2,1,0:T(8,128)(2,1)} fusion(bf16[256,256]{1,0:T(8,128)(2,1)S(1)} %fusion.3, bf16[2048,256]{1,0:T(8,128)(2,1)S(1)} %copy-done.2, bf16[32,8,2048]{2,1,0:T(8,128)(2,1)S(1)} %all-to-all-done, pred[256]{0:T(512)(128)(4,1)S(1)} %fusion.10), kind=kOutput, calls=%fused_computation.2 | convolution fusion | flops 268500992 | bytes 2359552 | tf_op jit(solution)/shard_map/dot_general | solution.py:211
  31.9 7.2 %all-to-all-start.1 = ((bf16[32,8,256]{2,1,0:T(8,128)(2,1)}), bf16[32,8,256]{2,1,0:T(8,128)(2,1)S(1)}, u32[]{:S(2)}, u32[]{:S(2)}) async-start(bf16[32,8,256]{2,1,0:T(8,128)(2,1)} %fusion.1), calls=%async_computation.1 | async-start | bytes 262144 | tf_op jit(solution)/shard_map/all_to_all | solution.py:216
  39.1 0.0 collective-permute-done.3
  39.1 0.7 %fusion.8 = bf16[8,16,64]{2,1,0:T(8,128)(2,1)} fusion(s32[]{:T(128)S(6)} %select_n.37, bf16[8,16,64]{2,1,0:T(8,128)(2,1)S(1)} %bitcast.33), kind=kLoop, calls=%fused_computation.12 | loop fusion | flops 8192 | bytes 32772 | tf_op jit(solution)/shard_map/jit(_roll_dynamic)/concatenate | solution.py:189
  39.8 2.9 %coarse.1 = f32[128,4096]{1,0:T(8,128)} custom-call(bf16[128,64]{1,0:T(8,128)(2,1)} %bitcast.31, s32[8,4096]{1,0:T(8,128)} %codes_ref.2, bf16[64,256]{1,0:T(8,128)(2,1)} %bitcast.34), custom_call_target="tpu_custom_call" | custom-call | flops 1000000 | bytes 100000 | tf_op jit(solution)/shard_map/coarse/pallas_call | solution.py:190
  42.7 4.0 %all-to-all-done.1 = bf16[32,8,256]{2,1,0:T(8,128)(2,1)S(1)} async-done(((bf16[32,8,256]{2,1,0:T(8,128)(2,1)}), bf16[32,8,256]{2,1,0:T(8,128)(2,1)S(1)}, u32[]{:S(2)}, u32[]{:S(2)}) %all-to-all-start.1) | async-done | bytes 131104 | tf_op jit(solution)/shard_map/all_to_all | solution.py:216
  46.7 0.0 copy-done
  46.7 0.8 %convolution_bitcast_fusion = f32[1,16,8,256]{3,2,1,0:T(8,128)} fusion(bf16[32,8,256]{2,1,0:T(8,128)(2,1)S(1)} %all-to-all-done.1, f32[128,256]{1,0:T(8,128)S(1)} %copy-done), kind=kOutput, calls=%fused_computation.3 | convolution fusion | flops 16809984 | bytes 393216 | tf_op jit(solution)/shard_map/dot_general | solution.py:219
  (9 shorter events, 0.1 us)
Async XLA Ops:
  3.2 8.7 %copy-start.1 = (bf16[16,64]{1,0:T(8,128)(2,1)S(1)}, bf16[16,64]{1,0:T(8,128)(2,1)}, u32[]{:S(2)}) copy-start(bf16[16,64]{1,0:T(8,128)(2,1)} %get-tuple-element.7) | copy-start | bytes 6148
  3.2 25.9 %all-to-all-start = ((bf16[32,8,2048]{2,1,0:T(8,128)(2,1)}), bf16[32,8,2048]{2,1,0:T(8,128)(2,1)S(1)}, u32[]{:S(2)}, u32[]{:S(2)}) async-start(bf16[32,8,2048]{2,1,0:T(8,128)(2,1)} %bitcast.30), calls=%async_computation | async-start | bytes 2097152 | tf_op jit(solution)/shard_map/all_to_all | solution.py:156
  11.9 9.8 %collective-permute-start = (bf16[16,64]{1,0:T(8,128)(2,1)S(1)}, bf16[16,64]{1,0:T(8,128)(2,1)S(1)}, u32[]{:S(2)}, u32[]{:S(2)}) collective-permute-start(bf16[16,64]{1,0:T(8,128)(2,1)S(1)} %copy-done.1), channel_id=1, source_target_pairs={{224,0},{0,32},{32,64},{64,96},{96,128},{128,160},{160,192},{192,2... | collective-permute-start | bytes 6152 | tf_op jit(solution)/shard_map/ppermute | solution.py:182
  13.6 8.1 %collective-permute-start.1 = (bf16[16,64]{1,0:T(8,128)(2,1)S(1)}, bf16[16,64]{1,0:T(8,128)(2,1)S(1)}, u32[]{:S(2)}, u32[]{:S(2)}) collective-permute-start(bf16[16,64]{1,0:T(8,128)(2,1)S(1)} %copy-done.1), channel_id=1, source_target_pairs={{32,0},{64,32},{96,64},{128,96},{160,128},{192,160},{224,192},{0,2... | collective-permute-start | bytes 6152 | tf_op jit(solution)/shard_map/ppermute | solution.py:182
  21.7 9.0 %copy-start.2 = (bf16[2048,256]{1,0:T(8,128)(2,1)S(1)}, bf16[2048,256]{1,0:T(8,128)(2,1)}, u32[]{:S(2)}) copy-start(bf16[2048,256]{1,0:T(8,128)(2,1)} %get-tuple-element.11) | copy-start | bytes 3145732
  21.8 5.6 %collective-permute-start.2 = (bf16[48,64]{1,0:T(8,128)(2,1)S(1)}, bf16[48,64]{1,0:T(8,128)(2,1)S(1)}, u32[]{:S(2)}, u32[]{:S(2)}) collective-permute-start(bf16[48,64]{1,0:T(8,128)(2,1)S(1)} %pad_maximum_fusion), channel_id=1, source_target_pairs={{160,0},{192,32},{224,64},{0,96},{32,128},{64,160},{96,192},{128,2... | collective-permute-start | bytes 18440 | tf_op jit(solution)/shard_map/ppermute | solution.py:182
  23.4 15.6 %collective-permute-start.3 = (bf16[32,64]{1,0:T(8,128)(2,1)S(1)}, bf16[32,64]{1,0:T(8,128)(2,1)S(1)}, u32[]{:S(2)}, u32[]{:S(2)}) collective-permute-start(bf16[32,64]{1,0:T(8,128)(2,1)S(1)} %pad_maximum_fusion.1), channel_id=1, source_target_pairs={{96,0},{128,32},{160,64},{192,96},{224,128},{0,160},{32,192},{64,2... | collective-permute-start | bytes 12296 | tf_op jit(solution)/shard_map/ppermute | solution.py:182
  30.8 15.9 %copy-start = (f32[128,256]{1,0:T(8,128)S(1)}, f32[128,256]{1,0:T(8,128)}, u32[]{:S(2)}) copy-start(f32[128,256]{1,0:T(8,128)} %get-tuple-element.8) | copy-start | bytes 393220
  31.9 14.8 %all-to-all-start.1 = ((bf16[32,8,256]{2,1,0:T(8,128)(2,1)}), bf16[32,8,256]{2,1,0:T(8,128)(2,1)S(1)}, u32[]{:S(2)}, u32[]{:S(2)}) async-start(bf16[32,8,256]{2,1,0:T(8,128)(2,1)} %fusion.1), calls=%async_computation.1 | async-start | bytes 262144 | tf_op jit(solution)/shard_map/all_to_all | solution.py:216

commit v5 on v4

--- a/solution.py
+++ b/solution.py
@@ -60,14 +60,16 @@
     routing = jnp.where(rank_at == turn, named_at, 0.0).astype(jnp.bfloat16)
     lane = lax.broadcasted_iota(jnp.int32, (count, LANES), 1)
     source = lane // 64 * 64 + lane % 8 * 8 + lane // 8 % 8
-    for first in range(0, width, LANES):
-        piece = queries_ref[:, first : first + LANES].astype(jnp.float32)
-        piece = jnp.take_along_axis(piece, source, axis=1).astype(jnp.bfloat16)
-        out_ref[:, first : first + LANES] = jnp.dot(
-            routing, piece, preferred_element_type=jnp.float32
+    for first in range(0, width, 4 * LANES):
+        pieces = []
+        for start in range(first, first + 4 * LANES, LANES):
+            piece = queries_ref[:, start : start + LANES].astype(jnp.float32)
+            pieces.append(jnp.take_along_axis(piece, source, axis=1).astype(jnp.bfloat16))
+        if first == 0:
+            prefix_ref[...] = pieces[0][:, :PREFIX]
+        out_ref[:, first : first + 4 * LANES] = jnp.dot(
+            routing, jnp.concatenate(pieces, axis=1), preferred_element_type=jnp.float32
         ).astype(jnp.bfloat16)
-        if first == 0:
-            prefix_ref[...] = piece[:, :PREFIX]
     slots = jnp.zeros(lists.shape, jnp.int32)
     for cluster in range(clusters):
         slots = jnp.where(lists == cluster, owner_ref[cluster], slots)

time: 47.9 us -> 47.9 us (level)
  no operation moved by 1% of the time
where the time goes in v5:
time: 47.9 us; the launch traced here: 47.5 us
  starting transfers between devices  26.2 us (55%)
  Pallas kernels  9.54 us (20%)
  waiting for transfers between devices  6.75 us (14%)
  matrix products  3.58 us (7%)
  between operations  0.72 us (2%)
  other arithmetic  0.7 us (1%)
    ppermute x4, starting transfers between devices, from_group(): return lax.ppermute(value, 'group', pairs)  10.3 us
    all_to_all x1, starting transfers between devices, body(): lax.all_to_all(outgoing.reshape(shards, positions // shards, width), 'sha...  8.72 us
    all_to_all x1, starting transfers between devices, body(): lax.all_to_all(computed.reshape(shards, positions // shards, row_count),...  7.16 us
    pallas_call x1, Pallas kernels, body(): pl.pallas_call(rebuild_kernel, grid=(subspaces // CHUNK,), in_specs=[pl.B...  4.06 us
    all_to_all x1, waiting for transfers between devices, body(): lax.all_to_all(computed.reshape(shards, positions // shards, row_count),...  4.01 us
    pallas_call x1, Pallas kernels, body(): pl.pallas_call(coarse_kernel, grid=(slab_rows // SPAN,), in_specs=[pl.Blo...  2.91 us
    dot_general x2, matrix products, body(): jnp.dot(arrived, columns, preferred_element_type=jnp.float32)  2.75 us
    pallas_call x1, Pallas kernels, body(): pl.pallas_call(route_kernel, in_specs=[whole, pl.BlockSpec(memory_space=p...  2.56 us
  transfers between devices with their start and end apart: 6, of which 3 were waited for; matrix products, arithmetic and copies ran while one was open for 7% of the time, Pallas kernels for 15%

profile of v5, /device:TPU:1, one launch (start us, length us, event | category | flops | bytes accessed | tf_op | source)
XLA Modules:
  0.0 47.5 jit_solution(3417282039121039345)
XLA Ops:
  0.6 2.6 %route.1 = (bf16[256,2048]{1,0:T(8,128)(2,1)}, bf16[16,64]{1,0:T(8,128)(2,1)}, f32[128,256]{1,0:T(8,128)}) custom-call(s32[1,64]{1,0:T(1,128)} %bitcast.36, s32[64]{0:T(128)} %owner_ref.1, s32[8,16]{1,0:T(8,128)} %bitcast.35, bf16[16,2048]{1,0:T(8,128)(2,1)} %bitcast.32), custom_call_target="tpu_custom_call" | custom-call | tf_op jit(solution)/shard_map/route/pallas_call | solution.py:148
  3.2 8.7 %all-to-all-start = ((bf16[32,8,2048]{2,1,0:T(8,128)(2,1)}), bf16[32,8,2048]{2,1,0:T(8,128)(2,1)S(1)}, u32[]{:S(2)}, u32[]{:S(2)}) async-start(bf16[32,8,2048]{2,1,0:T(8,128)(2,1)} %bitcast.30), calls=%async_computation | async-start | bytes 2097152 | tf_op jit(solution)/shard_map/all_to_all | solution.py:158
  11.9 0.0 copy-done.1
  11.9 1.7 %collective-permute-start = (bf16[16,64]{1,0:T(8,128)(2,1)S(1)}, bf16[16,64]{1,0:T(8,128)(2,1)S(1)}, u32[]{:S(2)}, u32[]{:S(2)}) collective-permute-start(bf16[16,64]{1,0:T(8,128)(2,1)S(1)} %copy-done.1), channel_id=1, source_target_pairs={{224,0},{0,32},{32,64},{64,96},{96,128},{128,160},{160,192},{192,2... | collective-permute-start | bytes 6152 | tf_op jit(solution)/shard_map/ppermute | solution.py:184
  13.6 4.0 %collective-permute-start.1 = (bf16[16,64]{1,0:T(8,128)(2,1)S(1)}, bf16[16,64]{1,0:T(8,128)(2,1)S(1)}, u32[]{:S(2)}, u32[]{:S(2)}) collective-permute-start(bf16[16,64]{1,0:T(8,128)(2,1)S(1)} %copy-done.1), channel_id=1, source_target_pairs={{32,0},{64,32},{96,64},{128,96},{160,128},{192,160},{224,192},{0,2... | collective-permute-start | bytes 6152 | tf_op jit(solution)/shard_map/ppermute | solution.py:184
  17.7 4.1 %rebuild.1 = (bf16[2048,256]{1,0:T(8,128)(2,1)}, bf16[2048,256]{1,0:T(8,128)(2,1)}) custom-call(s32[2]{0:T(128)} %counts_ref.1, s32[2,256,256]{2,1,0:T(8,128)} %codes_ref.3, bf16[256,2048]{1,0:T(8,128)(2,1)} %codebook_ref.1), custom_call_target="tpu_custom_call" | custom-call | flops 1000000 | bytes 100000 | tf_op jit(solution)/shard_map/rebuild/pallas_call | solution.py:165
  21.7 0.0 copy-start.2
  21.7 0.0 collective-permute-done
  21.8 0.0 collective-permute-done.1
  21.8 1.6 %collective-permute-start.2 = (bf16[48,64]{1,0:T(8,128)(2,1)S(1)}, bf16[48,64]{1,0:T(8,128)(2,1)S(1)}, u32[]{:S(2)}, u32[]{:S(2)}) collective-permute-start(bf16[48,64]{1,0:T(8,128)(2,1)S(1)} %pad_maximum_fusion), channel_id=1, source_target_pairs={{160,0},{192,32},{224,64},{0,96},{32,128},{64,160},{96,192},{128,2... | collective-permute-start | bytes 18440 | tf_op jit(solution)/shard_map/ppermute | solution.py:184
  23.4 2.9 %collective-permute-start.3 = (bf16[32,64]{1,0:T(8,128)(2,1)S(1)}, bf16[32,64]{1,0:T(8,128)(2,1)S(1)}, u32[]{:S(2)}, u32[]{:S(2)}) collective-permute-start(bf16[32,64]{1,0:T(8,128)(2,1)S(1)} %pad_maximum_fusion.1), channel_id=1, source_target_pairs={{96,0},{128,32},{160,64},{192,96},{224,128},{0,160},{32,192},{64,2... | collective-permute-start | bytes 12296 | tf_op jit(solution)/shard_map/ppermute | solution.py:184
  26.3 1.1 %collective-permute-done.2 = bf16[48,64]{1,0:T(8,128)(2,1)S(1)} collective-permute-done((bf16[48,64]{1,0:T(8,128)(2,1)S(1)}, bf16[48,64]{1,0:T(8,128)(2,1)S(1)}, u32[]{:S(2)}, u32[]{:S(2)}) %collective-permute-start.2) | collective-permute-done | bytes 6176 | tf_op jit(solution)/shard_map/ppermute | solution.py:184
  27.4 1.6 %all-to-all-done = bf16[32,8,2048]{2,1,0:T(8,128)(2,1)S(1)} async-done(((bf16[32,8,2048]{2,1,0:T(8,128)(2,1)}), bf16[32,8,2048]{2,1,0:T(8,128)(2,1)S(1)}, u32[]{:S(2)}, u32[]{:S(2)}) %all-to-all-start) | async-done | bytes 1048608 | tf_op jit(solution)/shard_map/all_to_all | solution.py:158
  29.1 1.7 %fusion.3 = bf16[256,256]{1,0:T(8,128)(2,1)S(1)} fusion(bf16[2048,256]{1,0:T(8,128)(2,1)} %get-tuple-element.10, bf16[32,8,2048]{2,1,0:T(8,128)(2,1)S(1)} %all-to-all-done), kind=kOutput, calls=%fused_computation.5 | convolution fusion | flops 268435456 | bytes 2228224 | tf_op jit(solution)/shard_map/dot_general | solution.py:213
  30.8 0.0 copy-done.2
  30.8 0.0 copy-start
  30.8 1.1 %fusion.1 = bf16[32,8,256]{2,1,0:T(8,128)(2,1)} fusion(bf16[256,256]{1,0:T(8,128)(2,1)S(1)} %fusion.3, bf16[2048,256]{1,0:T(8,128)(2,1)S(1)} %copy-done.2, bf16[32,8,2048]{2,1,0:T(8,128)(2,1)S(1)} %all-to-all-done, pred[256]{0:T(512)(128)(4,1)S(1)} %fusion.10), kind=kOutput, calls=%fused_computation.2 | convolution fusion | flops 268500992 | bytes 2359552 | tf_op jit(solution)/shard_map/dot_general | solution.py:213
  31.9 7.2 %all-to-all-start.1 = ((bf16[32,8,256]{2,1,0:T(8,128)(2,1)}), bf16[32,8,256]{2,1,0:T(8,128)(2,1)S(1)}, u32[]{:S(2)}, u32[]{:S(2)}) async-start(bf16[32,8,256]{2,1,0:T(8,128)(2,1)} %fusion.1), calls=%async_computation.1 | async-start | bytes 262144 | tf_op jit(solution)/shard_map/all_to_all | solution.py:218
  39.1 0.0 collective-permute-done.3
  39.1 0.7 %fusion.8 = bf16[8,16,64]{2,1,0:T(8,128)(2,1)} fusion(s32[]{:T(128)S(6)} %select_n.37, bf16[8,16,64]{2,1,0:T(8,128)(2,1)S(1)} %bitcast.33), kind=kLoop, calls=%fused_computation.12 | loop fusion | flops 8192 | bytes 32772 | tf_op jit(solution)/shard_map/jit(_roll_dynamic)/concatenate | solution.py:191
  39.8 2.9 %coarse.1 = f32[128,4096]{1,0:T(8,128)} custom-call(bf16[128,64]{1,0:T(8,128)(2,1)} %bitcast.31, s32[8,4096]{1,0:T(8,128)} %codes_ref.2, bf16[64,256]{1,0:T(8,128)(2,1)} %bitcast.34), custom_call_target="tpu_custom_call" | custom-call | flops 1000000 | bytes 100000 | tf_op jit(solution)/shard_map/coarse/pallas_call | solution.py:192
  42.7 4.0 %all-to-all-done.1 = bf16[32,8,256]{2,1,0:T(8,128)(2,1)S(1)} async-done(((bf16[32,8,256]{2,1,0:T(8,128)(2,1)}), bf16[32,8,256]{2,1,0:T(8,128)(2,1)S(1)}, u32[]{:S(2)}, u32[]{:S(2)}) %all-to-all-start.1) | async-done | bytes 131104 | tf_op jit(solution)/shard_map/all_to_all | solution.py:218
  46.7 0.0 copy-done
  46.7 0.8 %convolution_bitcast_fusion = f32[1,16,8,256]{3,2,1,0:T(8,128)} fusion(bf16[32,8,256]{2,1,0:T(8,128)(2,1)S(1)} %all-to-all-done.1, f32[128,256]{1,0:T(8,128)S(1)} %copy-done), kind=kOutput, calls=%fused_computation.3 | convolution fusion | flops 16809984 | bytes 393216 | tf_op jit(solution)/shard_map/dot_general | solution.py:221
  (9 shorter events, 0.1 us)
Async XLA Ops:
  3.2 8.7 %copy-start.1 = (bf16[16,64]{1,0:T(8,128)(2,1)S(1)}, bf16[16,64]{1,0:T(8,128)(2,1)}, u32[]{:S(2)}) copy-start(bf16[16,64]{1,0:T(8,128)(2,1)} %get-tuple-element.7) | copy-start | bytes 6148
  3.2 25.9 %all-to-all-start = ((bf16[32,8,2048]{2,1,0:T(8,128)(2,1)}), bf16[32,8,2048]{2,1,0:T(8,128)(2,1)S(1)}, u32[]{:S(2)}, u32[]{:S(2)}) async-start(bf16[32,8,2048]{2,1,0:T(8,128)(2,1)} %bitcast.30), calls=%async_computation | async-start | bytes 2097152 | tf_op jit(solution)/shard_map/all_to_all | solution.py:158
  11.9 9.8 %collective-permute-start = (bf16[16,64]{1,0:T(8,128)(2,1)S(1)}, bf16[16,64]{1,0:T(8,128)(2,1)S(1)}, u32[]{:S(2)}, u32[]{:S(2)}) collective-permute-start(bf16[16,64]{1,0:T(8,128)(2,1)S(1)} %copy-done.1), channel_id=1, source_target_pairs={{224,0},{0,32},{32,64},{64,96},{96,128},{128,160},{160,192},{192,2... | collective-permute-start | bytes 6152 | tf_op jit(solution)/shard_map/ppermute | solution.py:184
  13.6 8.1 %collective-permute-start.1 = (bf16[16,64]{1,0:T(8,128)(2,1)S(1)}, bf16[16,64]{1,0:T(8,128)(2,1)S(1)}, u32[]{:S(2)}, u32[]{:S(2)}) collective-permute-start(bf16[16,64]{1,0:T(8,128)(2,1)S(1)} %copy-done.1), channel_id=1, source_target_pairs={{32,0},{64,32},{96,64},{128,96},{160,128},{192,160},{224,192},{0,2... | collective-permute-start | bytes 6152 | tf_op jit(solution)/shard_map/ppermute | solution.py:184
  21.7 9.0 %copy-start.2 = (bf16[2048,256]{1,0:T(8,128)(2,1)S(1)}, bf16[2048,256]{1,0:T(8,128)(2,1)}, u32[]{:S(2)}) copy-start(bf16[2048,256]{1,0:T(8,128)(2,1)} %get-tuple-element.11) | copy-start | bytes 3145732
  21.8 5.6 %collective-permute-start.2 = (bf16[48,64]{1,0:T(8,128)(2,1)S(1)}, bf16[48,64]{1,0:T(8,128)(2,1)S(1)}, u32[]{:S(2)}, u32[]{:S(2)}) collective-permute-start(bf16[48,64]{1,0:T(8,128)(2,1)S(1)} %pad_maximum_fusion), channel_id=1, source_target_pairs={{160,0},{192,32},{224,64},{0,96},{32,128},{64,160},{96,192},{128,2... | collective-permute-start | bytes 18440 | tf_op jit(solution)/shard_map/ppermute | solution.py:184
  23.4 15.6 %collective-permute-start.3 = (bf16[32,64]{1,0:T(8,128)(2,1)S(1)}, bf16[32,64]{1,0:T(8,128)(2,1)S(1)}, u32[]{:S(2)}, u32[]{:S(2)}) collective-permute-start(bf16[32,64]{1,0:T(8,128)(2,1)S(1)} %pad_maximum_fusion.1), channel_id=1, source_target_pairs={{96,0},{128,32},{160,64},{192,96},{224,128},{0,160},{32,192},{64,2... | collective-permute-start | bytes 12296 | tf_op jit(solution)/shard_map/ppermute | solution.py:184
  30.8 15.9 %copy-start = (f32[128,256]{1,0:T(8,128)S(1)}, f32[128,256]{1,0:T(8,128)}, u32[]{:S(2)}) copy-start(f32[128,256]{1,0:T(8,128)} %get-tuple-element.8) | copy-start | bytes 393220
  31.9 14.8 %all-to-all-start.1 = ((bf16[32,8,256]{2,1,0:T(8,128)(2,1)}), bf16[32,8,256]{2,1,0:T(8,128)(2,1)S(1)}, u32[]{:S(2)}, u32[]{:S(2)}) async-start(bf16[32,8,256]{2,1,0:T(8,128)(2,1)} %fusion.1), calls=%async_computation.1 | async-start | bytes 262144 | tf_op jit(solution)/shard_map/all_to_all | solution.py:218
